TPU v7x, 32 devices: a whole 2x2x4 slice. The times are simulated.
32 devices in a mesh: head: 2 (over x), expert: 16 (over z, y, core).
Axes of the slice: x: 2, y: 2, z: 4, core: 2. Of those that a mesh axis runs over, the one named last changes fastest.
Arguments:
- q_latent: bfloat16 [128, 64, 512], P('expert', 'head'), may hold values from -16 to 16
- q_rotary: bfloat16 [128, 64, 64], P('expert', 'head'), may hold values from -3 to 3
- cache_latent: bfloat16 [128, 128, 512], P('expert'), may hold values from -5 to 5
- cache_rotary: bfloat16 [128, 64, 128], P('expert'), may hold values from -5 to 5
- lengths: int32 [128], P('expert'), may hold values from 16 to 128, as said below
- w_value_out: bfloat16 [32768, 5120], P('head', 'expert'), may hold values from -0.25 to 0.25
- resid: bfloat16 [128, 5120], P('expert'), may hold values from -8 to 8
- norm_gain: float32 [5120], replicated, may hold values from 0.1 to 1.9
- route_ids: int32 [128, 6], P('expert'), may hold values from 0 to 15, as said below
- route_weights: float32 [128, 6], P('expert'), may hold values from 0.1 to 0.6
- w_gate_up: bfloat16 [16, 2, 768, 5120], P('expert', None, 'head'), may hold values from -0.078125 to 0.078125
- w_down: bfloat16 [16, 768, 5120], P('expert', 'head'), may hold values from -0.21875 to 0.21875
Outputs:
- mixed_out: float32 [128, 5120], P('expert', 'head')
Inputs may be any that keep to these rules, and one draw needn't show every extreme that they name: `lengths`: slots at positions below a sequence's length are valid; some sequence has length 128. `route_ids`: each row names 6 different experts. Among the rows of one device (aligned blocks of 8 rows) no expert is named by more than 3 rows, and one expert is named by exactly 3 rows in every block.
All inputs are finite; a program needn't handle non-finite values.
Results may differ from a plain program's by a relative error of at most 0.0046.
Values may be sent and summed in bfloat16 or wider, within the bound.
A program may use at most 64 MiB of HBM per device.

v0:
```python
import jax
import jax.numpy as jnp
from jax import lax
from jax.sharding import PartitionSpec as P

softmax_scale = 192.0 ** (-0.5)
norm_epsilon = 1e-06


def attend(q_latent, q_rotary, cache_latent, cache_rotary, lengths):
    scores = jnp.einsum("shl,scl->shc", q_latent, cache_latent, preferred_element_type=jnp.float32)
    scores = scores + jnp.einsum(
        "shr,src->shc", q_rotary, cache_rotary, preferred_element_type=jnp.float32
    )
    scores = scores * softmax_scale
    position = lax.broadcasted_iota(jnp.int32, scores.shape, 2)
    scores = jnp.where(position < lengths[:, None, None], scores, -1e30)
    highest = jnp.max(scores, axis=2, keepdims=True)
    weights = jnp.exp(scores - highest)
    probs = (weights / jnp.sum(weights, axis=2, keepdims=True)).astype(jnp.bfloat16)
    return jnp.einsum(
        "shc,scl->shl", probs, cache_latent, preferred_element_type=jnp.float32
    ).astype(jnp.bfloat16)


def on_device(
    q_latent,
    q_rotary,
    cache_latent,
    cache_rotary,
    lengths,
    w_value_out,
    resid,
    norm_gain,
    route_ids,
    route_weights,
    w_gate_up,
    w_down,
):
    seq_local = q_latent.shape[0]
    latent_out = attend(q_latent, q_rotary, cache_latent, cache_rotary, lengths)
    flattened = latent_out.reshape(seq_local, -1)
    column_terms = jnp.dot(
        lax.all_gather(flattened, "expert", axis=0, tiled=True),
        w_value_out,
        preferred_element_type=jnp.float32,
    )
    column_sums = lax.psum(column_terms, "head")
    attention = lax.all_to_all(
        column_sums.astype(jnp.bfloat16), "expert", split_axis=0, concat_axis=1, tiled=True
    )
    stream = resid.astype(jnp.float32) + attention.astype(jnp.float32)
    mean_square = jnp.mean(stream * stream, axis=1, keepdims=True)
    normed = (stream * lax.rsqrt(mean_square + norm_epsilon) * norm_gain).astype(jnp.bfloat16)
    expert_count = lax.axis_size("expert")
    top_count = route_ids.shape[1]
    capacity = max(2, -(-(seq_local * top_count) // expert_count))
    flat_ids = route_ids.reshape(-1)
    one_hot = (flat_ids[:, None] == jnp.arange(expert_count, dtype=jnp.int32)[None, :]).astype(
        jnp.int32
    )
    earlier = jnp.cumsum(one_hot, axis=0) - one_hot
    slot_index = jnp.sum(earlier * one_hot, axis=1)
    target = (flat_ids * capacity + slot_index).reshape(seq_local, top_count)
    places = jnp.arange(expert_count * capacity, dtype=jnp.int32)
    matches = target[None, :, :] == places[:, None, None]
    selector = jnp.sum(matches.astype(jnp.int32), axis=2).astype(jnp.bfloat16)
    blending = jnp.sum(jnp.where(matches, route_weights[None, :, :], 0.0), axis=2)
    outgoing = jnp.dot(selector, normed, preferred_element_type=jnp.float32).astype(jnp.bfloat16)
    outgoing = outgoing.reshape(expert_count, capacity, -1)
    gate_up = w_gate_up[0]
    down_local = w_down[0]
    col_width = stream.shape[1] // lax.axis_size("head")
    offset = lax.axis_index("head") * col_width
    arrived = lax.all_to_all(outgoing, "expert", split_axis=0, concat_axis=0, tiled=True)
    flat_rows = arrived.reshape(-1, arrived.shape[2])
    projected = jnp.einsum("rd,gfd->rgf", flat_rows, gate_up, preferred_element_type=jnp.float32)
    hidden = (jax.nn.silu(projected[:, 0]) * projected[:, 1]).astype(jnp.bfloat16)
    partial_rows = jnp.dot(hidden, down_local, preferred_element_type=jnp.float32)
    expert_terms = partial_rows.reshape(arrived.shape[0], arrived.shape[1], -1)
    summed_rows = lax.psum(expert_terms.astype(jnp.bfloat16), "head")
    returned = lax.all_to_all(summed_rows, "expert", split_axis=0, concat_axis=0, tiled=True)
    back_rows = returned.reshape(expert_count * capacity, -1).astype(jnp.float32)
    mixture = jnp.dot(blending.T, back_rows, precision=lax.Precision.HIGHEST)
    mixed_full = stream + mixture
    return lax.dynamic_slice_in_dim(mixed_full, offset, col_width, 1)


def solution(mesh):
    placed = (
        P("expert", "head", None),
        P("expert", "head", None),
        P("expert", None, None),
        P("expert", None, None),
        P("expert"),
        P("head", "expert"),
        P("expert", None),
        P(),
        P("expert", None),
        P("expert", None),
        P("expert", None, "head", None),
        P("expert", "head", None),
    )
    return jax.shard_map(
        on_device, mesh=mesh, in_specs=placed, out_specs=P("expert", "head"), check_vma=False
    )
```

profile of v0, /device:TPU:0, one launch (start us, length us, event | category | flops | bytes accessed | tf_op | source)
XLA Modules:
  0.0 183.9 jit_solution(9629380776111968140)
XLA Ops:
  6.5 1.2 copy-done
  7.8 1.4 fusion.18
  9.1 1.1 fusion.8
  10.4 0.5 fusion.4
  10.9 0.8 copy.29
  11.8 0.8 eq.28
  13.0 52.2 %all-gather.2.cloned.1.call-done = bf16[128,16384]{1,0:T(8,128)(2,1)} async-done(((bf16[8,16384]{1,0:T(8,128)(2,1)}), bf16[128,16384]{1,0:T(8,128)(2,1)}) %all-gather.2.cloned.1.call-update) | async-done | bytes 4194320 | tf_op jit(solution)/shard_map/all_gather | solution.py:44
  65.2 6.8 %fusion.19 = f32[128,320]{0,1:T(8,128)S(1)} fusion(bf16[128,16384]{1,0:T(8,128)(2,1)} %all-gather.2.cloned.1.call-done, bf16[16384,320]{0,1:T(8,128)(2,1)} %param.17), kind=kOutput, calls=%fused_computation.38 | convolution fusion | flops 1342177280 | bytes 14843904 | tf_op jit(solution)/shard_map/dot_general | solution.py:43
  72.1 10.1 %all-reduce.4 = bf16[128,320]{0,1:T(8,128)(2,1)S(1)} all-reduce(f32[128,320]{0,1:T(8,128)S(1)} %fusion.19), channel_id=1, replica_groups=mesh['head'=2,'expert'=16] {'head'}, use_global_device_ids=true, to_apply=%region_2.3 | all-reduce | flops 40960 | bytes 245760 | tf_op jit(solution)/shard_map/psum | solution.py:48
  82.2 0.7 copy.23
  82.9 3.5 %all-to-all-start = ((bf16[16,8,320]{2,1,0:T(8,128)(2,1)}), bf16[16,8,320]{2,1,0:T(8,128)(2,1)S(1)}, u32[]{:S(2)}, u32[]{:S(2)}) async-start(bf16[16,8,320]{2,1,0:T(8,128)(2,1)} %bitcast), calls=%async_computation | async-start | bytes 196608 | tf_op jit(solution)/shard_map/all_to_all | solution.py:49
  86.7 7.1 %all-to-all-done = bf16[16,8,320]{2,1,0:T(8,128)(2,1)S(1)} async-done(((bf16[16,8,320]{2,1,0:T(8,128)(2,1)}), bf16[16,8,320]{2,1,0:T(8,128)(2,1)S(1)}, u32[]{:S(2)}, u32[]{:S(2)}) %all-to-all-start) | async-done | bytes 81952 | tf_op jit(solution)/shard_map/all_to_all | solution.py:49
  94.2 0.3 convolution_convert_fusion.1
  94.8 20.8 %all_to_all.23 = bf16[16,3,5120]{2,1,0:T(4,128)(2,1)S(1)} all-to-all(bf16[16,3,5120]{2,1,0:T(4,128)(2,1)S(1)} %reshape.44), channel_id=1, replica_groups=mesh['head'=2,'expert'=16] {'expert'}, dimensions={0} | all-to-all | bytes 983040 | tf_op jit(solution)/shard_map/all_to_all | solution.py:75
  115.6 0.4 reshape.48
  116.1 5.7 %fusion.1 = f32[48,2,384]{2,0,1:T(8,128)S(1)} fusion(bf16[48,5120,1]{1,0,2:T(8,128)(2,1)S(1)} %reshape.48, bf16[1,2,384,5120]{3,2,1,0:T(8,128)(2,1)} %param.22), kind=kOutput, calls=%fused_computation.1 | convolution fusion | flops 377487360 | bytes 8503296 | tf_op jit(solution)/shard_map/rd,gfd->rgf/dot_general | solution.py:77
  121.8 3.7 %convolution_convert_fusion = bf16[16,3,5120]{2,0,1:T(8,128)(2,1)} fusion(bf16[1,384,5120]{2,1,0:T(8,128)(2,1)} %param.23, bf16[16,3,384]{2,1,0:T(4,128)(2,1)S(1)} %convert_element_type.60), kind=kOutput, calls=%fused_computation.3 | convolution fusion | flops 188989440 | bytes 4460544 | tf_op jit(solution)/shard_map/dot_general | solution.py:79
  125.6 25.6 %all-reduce.3.cloned.1.call-done = bf16[16,3,5120]{2,0,1:T(8,128)(2,1)} async-done(((bf16[16,3,5120]{2,0,1:T(8,128)(2,1)}), bf16[16,3,5120]{2,0,1:T(8,128)(2,1)}) %all-reduce.3.cloned.1.call-update) | async-done | bytes 491536 | tf_op jit(solution)/shard_map/psum | solution.py:81
  151.2 2.3 %copy.28 = bf16[16,3,5120]{2,1,0:T(4,128)(2,1)} copy(bf16[16,3,5120]{2,0,1:T(8,128)(2,1)} %all-reduce.3.cloned.1.call-done) | data formatting | bytes 983040 | tf_op jit(solution)/shard_map/psum | solution.py:81
  153.5 5.6 %all-to-all-start.2 = ((bf16[16,3,5120]{2,1,0:T(4,128)(2,1)}), bf16[16,3,5120]{2,1,0:T(4,128)(2,1)S(1)}, u32[]{:S(2)}, u32[]{:S(2)}) async-start(bf16[16,3,5120]{2,1,0:T(4,128)(2,1)} %copy.28), calls=%async_computation.2 | async-start | bytes 1310720 | tf_op jit(solution)/shard_map/all_to_all | solution.py:82
  159.3 16.4 %all-to-all-done.2 = bf16[16,3,5120]{2,1,0:T(4,128)(2,1)S(1)} async-done(((bf16[16,3,5120]{2,1,0:T(4,128)(2,1)}), bf16[16,3,5120]{2,1,0:T(4,128)(2,1)S(1)}, u32[]{:S(2)}, u32[]{:S(2)}) %all-to-all-start.2) | async-done | bytes 491552 | tf_op jit(solution)/shard_map/all_to_all | solution.py:82
  175.7 0.4 reshape.46
  176.1 0.3 fusion.20
  176.4 0.7 dynamic-slice_add_fusion
  (31 shorter events, 1.7 us)
Async XLA Ops:
  6.5 1.2 copy-start
  6.5 58.7 %all-gather.2.cloned.1.call-start = ((), (), s32[]{:S(2)}) async-start(), calls=%async_computation.3 | async-start | bytes 4456448 | tf_op jit(solution)/shard_map/all_gather | solution.py:44
  13.0 73.5 %copy-start.3 = (s32[8,6]{1,0:T(8,128)S(1)}, s32[8,6]{1,0:T(8,128)}, u32[]{:S(2)}) copy-start(s32[8,6]{1,0:T(8,128)} %param.20) | copy-start | bytes 580
  13.0 81.0 %copy-start.1 = (bf16[8,5120]{1,0:T(8,128)(2,1)S(1)}, bf16[8,5120]{1,0:T(8,128)(2,1)}, u32[]{:S(2)}) copy-start(bf16[8,5120]{1,0:T(8,128)(2,1)} %param.18) | copy-start | bytes 245764
  13.0 81.2 %copy-start.2 = (f32[5120]{0:T(1024)S(1)}, f32[5120]{0:T(1024)}, u32[]{:S(2)}) copy-start(f32[5120]{0:T(1024)} %param.19) | copy-start | bytes 61444
  82.9 10.9 %all-to-all-start = ((bf16[16,8,320]{2,1,0:T(8,128)(2,1)}), bf16[16,8,320]{2,1,0:T(8,128)(2,1)S(1)}, u32[]{:S(2)}, u32[]{:S(2)}) async-start(bf16[16,8,320]{2,1,0:T(8,128)(2,1)} %bitcast), calls=%async_computation | async-start | bytes 196608 | tf_op jit(solution)/shard_map/all_to_all | solution.py:49
  86.5 64.7 %all-reduce.3.cloned.1.call-start = ((), (), s32[]{:S(2)}) async-start(), calls=%async_computation.4 | async-start | bytes 983040 | tf_op jit(solution)/shard_map/psum | solution.py:81
  116.0 43.1 %copy-start.4 = (f32[8,6]{1,0:T(8,128)S(1)}, f32[8,6]{1,0:T(8,128)}, u32[]{:S(2)}) copy-start(f32[8,6]{1,0:T(8,128)} %param.21) | copy-start | bytes 580
  153.5 22.2 %all-to-all-start.2 = ((bf16[16,3,5120]{2,1,0:T(4,128)(2,1)}), bf16[16,3,5120]{2,1,0:T(4,128)(2,1)S(1)}, u32[]{:S(2)}, u32[]{:S(2)}) async-start(bf16[16,3,5120]{2,1,0:T(4,128)(2,1)} %copy.28), calls=%async_computation.2 | async-start | bytes 1310720 | tf_op jit(solution)/shard_map/all_to_all | solution.py:82
Sparse Core Ops, SparseCore 0:
  11.9 53.2 all-gather.1
  125.7 25.4 all-reduce.2
where the time goes:
time: 184 us
  waiting for transfers between devices  101 us (55%)
  blocking collectives  30.9 us (17%)
  matrix products  19.8 us (11%)
  between operations  13.6 us (7%)
  starting transfers between devices  9.17 us (5%)
  local copies, waits for them, and re-layouts  7.41 us (4%)
    all_gather x1, waiting for transfers between devices, on_device(): lax.all_gather(flattened, 'expert', axis=0, tiled=True)  52.2 us
    psum x1, waiting for transfers between devices, on_device(): summed_rows = lax.psum(expert_terms.astype(jnp.bfloat16), 'head')  25.6 us
    all_to_all x1, blocking collectives, on_device(): lax.all_to_all(outgoing, 'expert', split_axis=0, concat_axis=0, tiled=True)  20.8 us
    all_to_all x1, waiting for transfers between devices, on_device(): lax.all_to_all(summed_rows, 'expert', split_axis=0, concat_axis=0, tiled=...  16.4 us
    psum x1, blocking collectives, on_device(): column_sums = lax.psum(column_terms, 'head')  10.1 us
    all_to_all x1, waiting for transfers between devices, on_device(): lax.all_to_all(column_sums.astype(jnp.bfloat16), 'expert', split_axis=0,...  7.14 us
    dot_general x1, matrix products, on_device(): jnp.dot(lax.all_gather(flattened, 'expert', axis=0, tiled=True), w_value_...  6.82 us
    dot_general x1, matrix products, on_device(): jnp.einsum('rd,gfd->rgf', flat_rows, gate_up, preferred_element_type=jnp....  5.7 us
  transfers between devices with their start and end apart: 4, of which 4 were waited for; matrix products, arithmetic and copies ran while one was open for 1% of the time, Pallas kernels for 0%

commit v1 on v0

--- a/solution.py
+++ b/solution.py
@@ -1,10 +1,375 @@
+import functools
+
 import jax
 import jax.numpy as jnp
 from jax import lax
+from jax.experimental import pallas as pl
+from jax.experimental.pallas import tpu as pltpu
 from jax.sharding import PartitionSpec as P
 
+MESH = pl.DeviceIdType.MESH
 softmax_scale = 192.0 ** (-0.5)
 norm_epsilon = 1e-06
+
+LINE, PAIR, CORE = 4, 2, 2
+CHUNKS = 4
+EXTRA = 128
+SLOTS = 4
+
+
+def rows_of(blocks):
+    n, r, c = blocks.shape
+    return blocks.astype(jnp.float32).reshape(n * r, c).astype(jnp.bfloat16)
+
+
+def blocks_of(rows, n):
+    return rows.reshape(n, rows.shape[0] // n, rows.shape[1]).astype(jnp.bfloat16)
+
+
+def spread(z, y, c, buffers, up, down, side, sib, recv):
+    def slot(zz, yy, cc):
+        return (zz * PAIR + yy) * CORE + cc
+
+    def copy(k, s, sems, index, target):
+        return pltpu.make_async_remote_copy(
+            src_ref=buffers.at[k, s],
+            dst_ref=buffers.at[k, s],
+            send_sem=sems.at[k, index],
+            recv_sem=recv.at[k, s],
+            device_id={"expert": target},
+            device_id_type=MESH,
+        )
+
+    def each_send(k, zz, act):
+        s = slot(zz, y, c)
+
+        @pl.when(jnp.logical_and(zz <= z, z < LINE - 1))
+        def _():
+            act(copy(k, s, up, zz, slot(z + 1, y, c)))
+
+        @pl.when(jnp.logical_and(zz >= z, z > 0))
+        def _():
+            act(copy(k, s, down, zz, slot(z - 1, y, c)))
+
+        act(copy(k, s, side, zz, slot(z, 1 - y, c)))
+        act(copy(k, s, sib, zz, slot(z, y, 1 - c)))
+
+    def arrived(k, s):
+        copy(k, s, sib, 0, slot(z, y, 1 - c)).wait_recv()
+
+    def at_distance(d, act):
+        if d == 0:
+            act(z)
+            return
+
+        @pl.when(z - d >= 0)
+        def _():
+            act(z - d)
+
+        @pl.when(z + d < LINE)
+        def _():
+            act(z + d)
+
+    def step(k, d):
+        def line(zz):
+            if d > 0:
+                arrived(k, slot(zz, y, c))
+            each_send(k, zz, lambda x: x.start())
+
+        def across(zz):
+            s = slot(zz, 1 - y, c)
+            arrived(k, s)
+            copy(k, s, sib, LINE + zz, slot(z, y, 1 - c)).start()
+
+        if d < LINE:
+            at_distance(d, line)
+        if d > 0:
+            at_distance(d - 1, across)
+
+    def finish(k):
+        def body(i, carry):
+            arrived(k, slot(lax.div(i, PAIR), lax.rem(i, PAIR), 1 - c))
+            return carry
+
+        lax.fori_loop(0, LINE * PAIR, body, 0)
+
+    def drain(k):
+        def body(zz, carry):
+            each_send(k, zz, lambda x: x.wait_send())
+            copy(k, slot(zz, 1 - y, c), sib, LINE + zz, slot(z, y, 1 - c)).wait_send()
+            return carry
+
+        lax.fori_loop(0, LINE, body, 0)
+
+    return step, finish, drain
+
+
+def layer_kernel(
+    latent_ref, resid_ref, gain_ref, ids_ref, weights_ref, wvo_hbm, wgu_hbm, wdn_hbm,
+    out_ref,
+    wvo, wgu, wdn, gathered, partial, partner, outgoing, incoming, stream,
+    tokens, rows_send, rows_recv, back_out, back_in,
+    w_sem, g_up, g_down, g_side, g_sib, g_recv, t_up, t_down, t_side, t_sib, t_recv,
+    x_sem, a_send, a_recv, b_send, b_recv,
+):
+    n = LINE * PAIR * CORE
+    h, me = lax.axis_index("head"), lax.axis_index("expert")
+    z, y, c = lax.div(me, PAIR * CORE), lax.rem(lax.div(me, CORE), PAIR), lax.rem(me, CORE)
+    seqs, width = resid_ref.shape
+    depth = gathered.shape[3]
+    cols = partial.shape[1]
+    half = out_ref.shape[1]
+    quarter = half // 2
+    top = ids_ref.shape[1]
+    capacity = rows_send.shape[0] // n
+    f32, bf16 = jnp.float32, jnp.bfloat16
+
+    loads = [
+        pltpu.make_async_copy(src, dst, w_sem.at[i])
+        for i, (src, dst) in enumerate(((wvo_hbm, wvo), (wgu_hbm, wgu), (wdn_hbm, wdn)))
+    ]
+    for load in loads:
+        load.start()
+
+    barrier = pltpu.get_barrier_semaphore()
+
+    def greet(o, carry):
+        pl.semaphore_signal(
+            barrier, inc=1, device_id={"expert": lax.rem(me + o, n)}, device_id_type=MESH
+        )
+        return carry
+
+    lax.fori_loop(1, n, greet, 0)
+    pl.semaphore_signal(barrier, inc=1, device_id={"head": 1 - h}, device_id_type=MESH)
+
+    for k in range(CHUNKS):
+        gathered[k, me] = latent_ref[:, k * depth : (k + 1) * depth]
+    partial[...] = jnp.zeros_like(partial)
+    pl.semaphore_wait(barrier, n)
+
+    step, finish, drain = spread(z, y, c, gathered, g_up, g_down, g_side, g_sib, g_recv)
+    tile = depth // 4
+
+    def turn(t, carry):
+        for d in range(LINE, -1, -1):
+            k = t - d
+
+            @pl.when(jnp.logical_and(k >= 0, k < CHUNKS))
+            def _():
+                step(k, d)
+
+        @pl.when(t == LINE)
+        def _():
+            loads[0].wait()
+
+        @pl.when(t >= LINE)
+        def _():
+            k = t - LINE
+            finish(k)
+            for j in range(4):
+                x = rows_of(gathered[k, :, :, j * tile : (j + 1) * tile])
+                w = wvo[pl.ds(pl.multiple_of(k * depth + j * tile, tile), tile), :]
+                partial[...] += jnp.dot(x, w, preferred_element_type=f32)
+
+        return carry
+
+    lax.fori_loop(0, CHUNKS + LINE, turn, 0)
+
+    swap = pltpu.make_async_remote_copy(
+        src_ref=partial, dst_ref=partner, send_sem=x_sem.at[0], recv_sem=x_sem.at[1],
+        device_id={"head": 1 - h}, device_id_type=MESH,
+    )
+    swap.start()
+    swap.wait_recv()
+    outgoing[...] = blocks_of(partial[...] + partner[...], n)
+
+    def owner(o, source, target, send, recv):
+        to = lax.rem(me + o, n)
+        return pltpu.make_async_remote_copy(
+            src_ref=source.at[to], dst_ref=target.at[me], send_sem=send.at[to],
+            recv_sem=recv.at[me], device_id={"expert": to}, device_id_type=MESH,
+        )
+
+    def exchange_start(source, target, send, recv):
+        def body(o, carry):
+            owner(o, source, target, send, recv).start()
+            return carry
+
+        lax.fori_loop(1, n, body, 0)
+
+    def exchange_recv(source, target, send, recv):
+        def body(o, carry):
+            who = lax.rem(me + o, n)
+            pltpu.make_async_remote_copy(
+                src_ref=source.at[who], dst_ref=target.at[who], send_sem=send.at[who],
+                recv_sem=recv.at[who], device_id={"expert": who}, device_id_type=MESH,
+            ).wait_recv()
+            return carry
+
+        lax.fori_loop(1, n, body, 0)
+
+    def exchange_sent(source, target, send, recv):
+        def body(o, carry):
+            owner(o, source, target, send, recv).wait_send()
+            return carry
+
+        lax.fori_loop(1, n, body, 0)
+
+    exchange_start(outgoing, incoming, a_send, a_recv)
+    incoming[me] = outgoing[me]
+    ids = ids_ref[...]
+    lane = lax.broadcasted_iota(jnp.int32, (seqs, EXTRA), 1)
+    named = jnp.zeros((seqs, EXTRA), f32)
+    for k in range(top):
+        named = named + jnp.where(ids[:, k : k + 1] == lane, 1.0, 0.0)
+    exchange_recv(outgoing, incoming, a_send, a_recv)
+
+    for e in range(n):
+        stream[:, e * cols : (e + 1) * cols] = incoming[e].astype(f32)
+    rows = stream[...] + resid_ref[...].astype(f32)
+    stream[...] = rows
+    mean_square = jnp.sum(rows * rows, axis=1, keepdims=True) * (1.0 / width)
+    normed = rows * lax.rsqrt(mean_square + norm_epsilon) * gain_ref[...]
+    tokens[0, me, :, :width] = normed.astype(bf16)
+    tokens[0, me, :, width:] = named.astype(bf16)
+
+    t_step, t_finish, t_drain = spread(z, y, c, tokens, t_up, t_down, t_side, t_sib, t_recv)
+    for d in range(LINE + 1):
+        t_step(0, d)
+
+    wide = n * 2 * SLOTS
+    place = lax.broadcasted_iota(jnp.int32, (seqs, wide), 1)
+    which, part, at = place // (2 * SLOTS), (place // SLOTS) % 2, place % SLOTS
+    hit = jnp.zeros((seqs, wide), f32)
+    share = jnp.zeros((seqs, wide), f32)
+    for k in range(top):
+        same = ids[:, k : k + 1] == which
+        hit = hit + jnp.where(same, 1.0, 0.0)
+        share = share + jnp.where(same, weights_ref[:, k : k + 1], 0.0)
+    token = lax.broadcasted_iota(jnp.int32, (seqs, wide), 0)
+    rank = jnp.zeros((seqs, wide), f32)
+    for t in range(seqs - 1):
+        rank = rank + jnp.where(token > t, hit[t : t + 1, :], 0.0)
+    blend = jnp.where(rank == at.astype(f32), share, 0.0)
+
+    t_finish(0)
+    loads[1].wait()
+
+    total = n * seqs
+    flags = rows_of(tokens[0, :, :, width:])
+    mine = jnp.where(lax.broadcasted_iota(jnp.int32, (8, EXTRA), 1) == me, 1.0, 0.0).astype(bf16)
+    chosen = lax.dot_general(mine, flags, (((1,), (1,)), ((), ())), preferred_element_type=f32)
+    first = lax.broadcasted_iota(jnp.int32, (total, total), 0)
+    second = lax.broadcasted_iota(jnp.int32, (total, total), 1)
+    ahead = jnp.where(
+        jnp.logical_and(first < second, first // seqs == second // seqs), 1.0, 0.0
+    ).astype(bf16)
+    order = jnp.dot(chosen.astype(bf16), ahead, preferred_element_type=f32)
+    count = capacity * n
+    row = lax.broadcasted_iota(jnp.int32, (count, total), 0)
+    tok = lax.broadcasted_iota(jnp.int32, (count, total), 1)
+    fits = jnp.logical_and(order[0:1, :] == (row // n).astype(f32), tok // seqs == row % n)
+    pick = jnp.where(fits, chosen[0:1, :], 0.0).astype(bf16)
+
+    units = wgu.shape[1]
+    gate = jnp.zeros((count, units), f32)
+    lift = jnp.zeros((count, units), f32)
+    span = width // 5
+    for j in range(5):
+        piece = slice(j * span, (j + 1) * span)
+        x = jnp.dot(pick, rows_of(tokens[0, :, :, piece]), preferred_element_type=f32).astype(bf16)
+        gate += lax.dot_general(
+            x, wgu[0, :, piece], (((1,), (1,)), ((), ())), preferred_element_type=f32
+        )
+        lift += lax.dot_general(
+            x, wgu[1, :, piece], (((1,), (1,)), ((), ())), preferred_element_type=f32
+        )
+    hidden = (gate / (1.0 + jnp.exp(-gate)) * lift).astype(bf16)
+    loads[2].wait()
+    theirs = pl.ds(pl.multiple_of((1 - h) * half, half), half)
+    ours = pl.ds(pl.multiple_of(h * half, half), half)
+    rows_send[...] = jnp.dot(hidden, wdn[:, theirs], preferred_element_type=f32).astype(bf16)
+    trade = pltpu.make_async_remote_copy(
+        src_ref=rows_send, dst_ref=rows_recv, send_sem=x_sem.at[2], recv_sem=x_sem.at[3],
+        device_id={"head": 1 - h}, device_id_type=MESH,
+    )
+    trade.start()
+    own = jnp.dot(hidden, wdn[:, ours], preferred_element_type=f32)
+    dest = lax.broadcasted_iota(jnp.int32, (n * 2 * SLOTS, count), 0)
+    from_row = lax.broadcasted_iota(jnp.int32, (n * 2 * SLOTS, count), 1)
+    home = from_row == (dest % SLOTS) * n + dest // (2 * SLOTS)
+    upper = (dest // SLOTS) % 2
+    trade.wait_recv()
+    summed = (own + rows_recv[...].astype(f32)).astype(bf16)
+    back = jnp.zeros((n * 2 * SLOTS, quarter), f32)
+    for a in range(2):
+        put = jnp.where(jnp.logical_and(home, upper == a), 1.0, 0.0).astype(bf16)
+        back += jnp.dot(put, summed[:, a * quarter : (a + 1) * quarter], preferred_element_type=f32)
+    back_out[...] = blocks_of(back, n)
+    exchange_start(back_out, back_in, b_send, b_recv)
+    back_in[me] = back_out[me]
+    exchange_recv(back_out, back_in, b_send, b_recv)
+
+    returned = rows_of(back_in[...])
+    for a in range(2):
+        mix = jnp.where(part == a, blend, 0.0)
+        high = mix.astype(bf16)
+        low = (mix - high.astype(f32)).astype(bf16)
+        added = jnp.dot(high, returned, preferred_element_type=f32)
+        added = added + jnp.dot(low, returned, preferred_element_type=f32)
+        start = pl.multiple_of(h * half + a * quarter, quarter)
+        out_ref[:, a * quarter : (a + 1) * quarter] = stream[:, pl.ds(start, quarter)] + added
+
+    for k in range(CHUNKS):
+        drain(k)
+    t_drain(0)
+    swap.wait_send()
+    trade.wait_send()
+    exchange_sent(outgoing, incoming, a_send, a_recv)
+    exchange_sent(back_out, back_in, b_send, b_recv)
+
+
+def fused(latents, resid, norm_gain, route_ids, route_weights, w_value_out, w_gate_up, w_down):
+    n = LINE * PAIR * CORE
+    seqs, width = resid.shape
+    depth = latents.shape[1] // CHUNKS
+    cols = w_value_out.shape[1]
+    half = width // 2
+    capacity = -(-(seqs * route_ids.shape[1]) // n)
+    gate_up, down = w_gate_up[0], w_down[0]
+    bf16, f32 = jnp.bfloat16, jnp.float32
+    vmem, anywhere = pl.BlockSpec(memory_space=pltpu.VMEM), pl.BlockSpec(memory_space=pl.ANY)
+    dma = pltpu.SemaphoreType.DMA
+    return pl.pallas_call(
+        layer_kernel,
+        out_shape=jax.ShapeDtypeStruct((seqs, half), f32),
+        in_specs=[vmem] * 5 + [anywhere] * 3,
+        out_specs=vmem,
+        scratch_shapes=[
+            pltpu.VMEM(w_value_out.shape, bf16),
+            pltpu.VMEM(gate_up.shape, bf16),
+            pltpu.VMEM(down.shape, bf16),
+            pltpu.VMEM((CHUNKS, n, seqs, depth), bf16),
+            pltpu.VMEM((n * seqs, cols), f32),
+            pltpu.VMEM((n * seqs, cols), f32),
+            pltpu.VMEM((n, seqs, cols), bf16),
+            pltpu.VMEM((n, seqs, cols), bf16),
+            pltpu.VMEM((seqs, width), f32),
+            pltpu.VMEM((1, n, seqs, width + EXTRA), bf16),
+            pltpu.VMEM((capacity * n, half), bf16),
+            pltpu.VMEM((capacity * n, half), bf16),
+            pltpu.VMEM((n, 2 * SLOTS, half // 2), bf16),
+            pltpu.VMEM((n, 2 * SLOTS, half // 2), bf16),
+            dma((3,)),
+            dma((CHUNKS, LINE)), dma((CHUNKS, LINE)), dma((CHUNKS, LINE)),
+            dma((CHUNKS, PAIR * LINE)), dma((CHUNKS, n)),
+            dma((1, LINE)), dma((1, LINE)), dma((1, LINE)), dma((1, PAIR * LINE)), dma((1, n)),
+            dma((4,)), dma((n,)), dma((n,)), dma((n,)), dma((n,)),
+        ],
+        compiler_params=pltpu.CompilerParams(
+            collective_id=0, has_side_effects=True, vmem_limit_bytes=56 * 1024 * 1024
+        ),
+    )(latents, resid, norm_gain[None, :], route_ids, route_weights, w_value_out, gate_up, down)
 
 
 def attend(q_latent, q_rotary, cache_latent, cache_rotary, lengths):
@@ -40,6 +405,14 @@
     seq_local = q_latent.shape[0]
     latent_out = attend(q_latent, q_rotary, cache_latent, cache_rotary, lengths)
     flattened = latent_out.reshape(seq_local, -1)
+    if (
+        lax.axis_size("head") == 2
+        and lax.axis_size("expert") == LINE * PAIR * CORE
+        and seq_local == 8
+    ):
+        return fused(
+            flattened, resid, norm_gain, route_ids, route_weights, w_value_out, w_gate_up, w_down
+        )
     column_terms = jnp.dot(
         lax.all_gather(flattened, "expert", axis=0, tiled=True),
         w_value_out,

time: 184 us -> 107 us (0.58)
  waiting for transfers between devices: 101 us -> 0 us
  Pallas kernels: 0 us -> 83.9 us
  blocking collectives: 30.9 us -> 0 us
  matrix products: 19.8 us -> 2.97 us
  between operations: 13.6 us -> 0.03 us
  local copies, waits for them, and re-layouts: 7.41 us -> 18.6 us
  starting transfers between devices: 9.17 us -> 0 us
    pallas_call x0 -> x1, Pallas kernels: none -> 83.9 us  [fused(): pl.pallas_call(layer_kernel, out_shape=jax.ShapeDtypeStruct((seqs, half),...]
    all_gather x1 -> x0, waiting for transfers between devices: 52.2 us -> none  [on_device(): lax.all_gather(flattened, 'expert', axis=0, tiled=True)]
    psum x1 -> x0, waiting for transfers between devices: 25.6 us -> none  [on_device(): summed_rows = lax.psum(expert_terms.astype(jnp.bfloat16), 'head')]
    all_to_all x2 -> x0, waiting for transfers between devices: 23.6 us -> none  [the longest x1 16.4 us: on_device(): lax.all_to_all(summed_rows, 'expert', split_axis=0, concat_axis=0, tiled=...]
    all_to_all x1 -> x0, blocking collectives: 20.8 us -> none  [on_device(): lax.all_to_all(outgoing, 'expert', split_axis=0, concat_axis=0, tiled=True)]
    dot_general x5 -> x0, matrix products: 16.9 us -> none  [the longest x1 6.82 us: on_device(): jnp.dot(lax.all_gather(flattened, 'expert', axis=0, tiled=True), w_value_...]
    unnamed x12 -> x5, local copies, waits for them, and re-layouts: 2.18 us -> 18.6 us
    psum x1 -> x0, blocking collectives: 10.1 us -> none  [on_device(): column_sums = lax.psum(column_terms, 'head')]
  transfers between devices with their start and end apart: 4 -> 0, of which waited for: 4 -> 0; matrix products, arithmetic and copies ran while one was open for 1% -> 0% of each run, Pallas kernels for 0% -> 0%
where the time goes in v1:
time: 107 us; the launch traced here: 106 us
  Pallas kernels  83.9 us (78%)
  local copies, waits for them, and re-layouts  18.6 us (17%)
  matrix products  2.97 us (3%)
    pallas_call x1, Pallas kernels, fused(): pl.pallas_call(layer_kernel, out_shape=jax.ShapeDtypeStruct((seqs, half),...  83.9 us
    unnamed x5, local copies, waits for them, and re-layouts  18.6 us

profile of v1, /device:TPU:0, one launch (start us, length us, event | category | flops | bytes accessed | tf_op | source)
XLA Modules:
  0.0 105.7 jit_solution(12611974946692050945)
XLA Ops:
  0.0 0.0 copy-start
  0.0 1.2 %copy-done = bf16[8,128,512]{2,1,0:T(8,128)(2,1)S(1)} copy-done((bf16[8,128,512]{2,1,0:T(8,128)(2,1)S(1)}, bf16[8,128,512]{2,1,0:T(8,128)(2,1)}, u32[]{:S(2)}) %copy-start) | copy-done | bytes 1048600
  1.2 1.4 %fusion.9 = f32[8,32,128]{2,1,0:T(8,128)S(1)} fusion(bf16[8,32,512]{2,1,0:T(8,128)(2,1)} %param.12, bf16[8,128,512]{2,1,0:T(8,128)(2,1)S(1)} %copy-done), kind=kOutput, calls=%fused_computation.13 | convolution fusion | flops 33554432 | bytes 1441792 | tf_op jit(solution)/shard_map/shl,scl->shc/dot_general | solution.py:376
  2.6 1.1 %fusion.5 = f32[8,32,128]{2,1,0:T(8,128)S(1)} fusion(f32[8,32,128]{2,1,0:T(8,128)S(1)} %fusion.9, bf16[8,32,64]{2,1,0:T(8,128)(2,1)} %param.13, bf16[8,64,128]{2,1,0:T(8,128)(2,1)} %param.15, s32[8]{0:T(128)} %param.16), kind=kOutput, calls=%fused_computation.7 | convolution fusion | flops 4325376 | bytes 426016 | tf_op jit(solution)/shard_map/shr,src->shc/dot_general | solution.py:377
  3.7 0.2 fusion.8
  3.9 0.5 fusion.1
  4.4 0.9 copy.14
  5.3 15.0 %copy.13.wvo_hbm = bf16[16384,320]{1,0:T(8,128)(2,1)} copy(bf16[16384,320]{0,1:T(8,128)(2,1)} %param.17) | data formatting | bytes 20971520 | tf_op args[5]
  20.3 83.9 %shard_map.118 = f32[8,2560]{1,0:T(8,128)} custom-call(bf16[8,16384]{1,0:T(8,128)(2,1)} %bitcast.15, bf16[8,5120]{1,0:T(8,128)(2,1)} %resid_ref.1, f32[1,5120]{1,0:T(1,128)} %bitcast.16, s32[8,6]{1,0:T(8,128)} %ids_ref.1, f32[8,6]{1,0:T(8,128)} %weights_ref.1, bf16[16384,320]{1,0:T(8,128)(2,1)} %copy.13.wvo_hbm, bf16[2,384,5120]{2,1,0:T(8,128)(2,1)} %bitcast.13, ...), custom_call_target="tpu_custom_call" | custom-call | tf_op jit(solution)/shard_map/pallas_call | solution.py:343
  104.1 1.5 %copy.16 = f32[8,2560]{1,0:T(8,128)} copy(f32[8,2560]{1,0:T(8,128)} %shard_map.118) | data formatting | bytes 163840
Async XLA Ops:
  0.0 1.2 %copy-start = (bf16[8,128,512]{2,1,0:T(8,128)(2,1)S(1)}, bf16[8,128,512]{2,1,0:T(8,128)(2,1)}, u32[]{:S(2)}) copy-start(bf16[8,128,512]{2,1,0:T(8,128)(2,1)} %param.14) | copy-start | bytes 3145732

commit v2 on v1

--- a/solution.py
+++ b/solution.py
@@ -15,6 +15,7 @@
 CHUNKS = 4
 EXTRA = 128
 SLOTS = 4
+PARTS = 2
 
 
 def rows_of(blocks):
@@ -105,23 +106,24 @@
 
 
 def layer_kernel(
-    latent_ref, resid_ref, gain_ref, ids_ref, weights_ref, wvo_hbm, wgu_hbm, wdn_hbm,
+    q_ref, qr_ref, cache_ref, rot_ref, len_ref, resid_ref, gain_ref, ids_ref, weights_ref, wvo_hbm, wgu_hbm, wdn_hbm,
     out_ref,
-    wvo, wgu, wdn, gathered, partial, partner, outgoing, incoming, stream,
+    wvo, wgu, wdn, heads, gathered, partial, partner, outgoing, incoming, stream,
     tokens, rows_send, rows_recv, back_out, back_in,
     w_sem, g_up, g_down, g_side, g_sib, g_recv, t_up, t_down, t_side, t_sib, t_recv,
-    x_sem, a_send, a_recv, b_send, b_recv,
+    x_sem, y_send, y_recv, a_send, a_recv, b_send, b_recv,
 ):
     n = LINE * PAIR * CORE
     h, me = lax.axis_index("head"), lax.axis_index("expert")
     z, y, c = lax.div(me, PAIR * CORE), lax.rem(lax.div(me, CORE), PAIR), lax.rem(me, CORE)
     seqs, width = resid_ref.shape
-    depth = gathered.shape[3]
+    per_chunk, latent = gathered.shape[2], gathered.shape[4]
     cols = partial.shape[1]
     half = out_ref.shape[1]
-    quarter = half // 2
+    piece = half // (PARTS * 2)
+    span = width // PARTS
     top = ids_ref.shape[1]
-    capacity = rows_send.shape[0] // n
+    capacity = rows_send.shape[1] // n
     f32, bf16 = jnp.float32, jnp.bfloat16
 
     loads = [
@@ -142,17 +144,30 @@
     lax.fori_loop(1, n, greet, 0)
     pl.semaphore_signal(barrier, inc=1, device_id={"head": 1 - h}, device_id_type=MESH)
 
+    count = q_ref.shape[1]
+    slot = lax.broadcasted_iota(jnp.int32, (count, cache_ref.shape[1]), 1)
+    for s in range(seqs):
+        cache = cache_ref[s]
+        scores = lax.dot_general(
+            q_ref[s], cache, (((1,), (1,)), ((), ())), preferred_element_type=f32
+        )
+        scores = scores + jnp.dot(qr_ref[s], rot_ref[s], preferred_element_type=f32)
+        scores = jnp.where(slot < len_ref[s : s + 1, :], scores * softmax_scale, -1e30)
+        raised = jnp.exp(scores - jnp.max(scores, axis=1, keepdims=True))
+        probs = (raised / jnp.sum(raised, axis=1, keepdims=True)).astype(bf16)
+        heads[:, s, :] = jnp.dot(probs, cache, preferred_element_type=f32)
     for k in range(CHUNKS):
-        gathered[k, me] = latent_ref[:, k * depth : (k + 1) * depth]
+        gathered[k, me] = heads[k * per_chunk : (k + 1) * per_chunk].astype(bf16)
     partial[...] = jnp.zeros_like(partial)
     pl.semaphore_wait(barrier, n)
 
     step, finish, drain = spread(z, y, c, gathered, g_up, g_down, g_side, g_sib, g_recv)
-    tile = depth // 4
+    step(0, 0)
+    step(1, 0)
 
     def turn(t, carry):
         for d in range(LINE, -1, -1):
-            k = t - d
+            k = t - d if d else t + 1
 
             @pl.when(jnp.logical_and(k >= 0, k < CHUNKS))
             def _():
@@ -166,14 +181,19 @@
         def _():
             k = t - LINE
             finish(k)
-            for j in range(4):
-                x = rows_of(gathered[k, :, :, j * tile : (j + 1) * tile])
-                w = wvo[pl.ds(pl.multiple_of(k * depth + j * tile, tile), tile), :]
-                partial[...] += jnp.dot(x, w, preferred_element_type=f32)
+            for j in range(0, per_chunk, 2):
+                x = jnp.concatenate(
+                    [rows_of(gathered[k, :, j]), rows_of(gathered[k, :, j + 1])], axis=1
+                )
+                start = pl.multiple_of((k * per_chunk + j) * latent, 2 * latent)
+                partial[...] += lax.dot_general(
+                    x, wvo[:, pl.ds(start, 2 * latent)], (((1,), (1,)), ((), ())),
+                    preferred_element_type=f32,
+                )
 
         return carry
 
-    lax.fori_loop(0, CHUNKS + LINE, turn, 0)
+    lax.fori_loop(1, CHUNKS + LINE, turn, 0)
 
     swap = pltpu.make_async_remote_copy(
         src_ref=partial, dst_ref=partner, send_sem=x_sem.at[0], recv_sem=x_sem.at[1],
@@ -230,12 +250,14 @@
     stream[...] = rows
     mean_square = jnp.sum(rows * rows, axis=1, keepdims=True) * (1.0 / width)
     normed = rows * lax.rsqrt(mean_square + norm_epsilon) * gain_ref[...]
-    tokens[0, me, :, :width] = normed.astype(bf16)
-    tokens[0, me, :, width:] = named.astype(bf16)
+    for k in range(PARTS):
+        tokens[k, me, :, :span] = normed[:, k * span : (k + 1) * span].astype(bf16)
+        tokens[k, me, :, span:] = named.astype(bf16)
 
     t_step, t_finish, t_drain = spread(z, y, c, tokens, t_up, t_down, t_side, t_sib, t_recv)
     for d in range(LINE + 1):
-        t_step(0, d)
+        for k in range(PARTS):
+            t_step(k, d)
 
     wide = n * 2 * SLOTS
     place = lax.broadcasted_iota(jnp.int32, (seqs, wide), 1)
@@ -256,7 +278,7 @@
     loads[1].wait()
 
     total = n * seqs
-    flags = rows_of(tokens[0, :, :, width:])
+    flags = rows_of(tokens[0, :, :, span:])
     mine = jnp.where(lax.broadcasted_iota(jnp.int32, (8, EXTRA), 1) == me, 1.0, 0.0).astype(bf16)
     chosen = lax.dot_general(mine, flags, (((1,), (1,)), ((), ())), preferred_element_type=f32)
     first = lax.broadcasted_iota(jnp.int32, (total, total), 0)
@@ -274,65 +296,83 @@
     units = wgu.shape[1]
     gate = jnp.zeros((count, units), f32)
     lift = jnp.zeros((count, units), f32)
-    span = width // 5
-    for j in range(5):
-        piece = slice(j * span, (j + 1) * span)
-        x = jnp.dot(pick, rows_of(tokens[0, :, :, piece]), preferred_element_type=f32).astype(bf16)
-        gate += lax.dot_general(
-            x, wgu[0, :, piece], (((1,), (1,)), ((), ())), preferred_element_type=f32
-        )
-        lift += lax.dot_general(
-            x, wgu[1, :, piece], (((1,), (1,)), ((), ())), preferred_element_type=f32
-        )
+    for k in range(PARTS):
+        if k > 0:
+            t_finish(k)
+        for j in range(2):
+            lanes = slice(j * span // 2, (j + 1) * span // 2)
+            deep = slice(k * span + j * span // 2, k * span + (j + 1) * span // 2)
+            x = jnp.dot(pick, rows_of(tokens[k, :, :, lanes]), preferred_element_type=f32)
+            x = x.astype(bf16)
+            gate += lax.dot_general(
+                x, wgu[0, :, deep], (((1,), (1,)), ((), ())), preferred_element_type=f32
+            )
+            lift += lax.dot_general(
+                x, wgu[1, :, deep], (((1,), (1,)), ((), ())), preferred_element_type=f32
+            )
     hidden = (gate / (1.0 + jnp.exp(-gate)) * lift).astype(bf16)
     loads[2].wait()
-    theirs = pl.ds(pl.multiple_of((1 - h) * half, half), half)
+    share_cols = half // PARTS
+
+    def trade(p):
+        return pltpu.make_async_remote_copy(
+            src_ref=rows_send.at[p], dst_ref=rows_recv.at[p], send_sem=y_send.at[p],
+            recv_sem=y_recv.at[p], device_id={"head": 1 - h}, device_id_type=MESH,
+        )
+
+    for p in range(PARTS):
+        theirs = pl.ds(pl.multiple_of((1 - h) * half + p * share_cols, share_cols), share_cols)
+        rows_send[p] = jnp.dot(hidden, wdn[:, theirs], preferred_element_type=f32).astype(bf16)
+        trade(p).start()
     ours = pl.ds(pl.multiple_of(h * half, half), half)
-    rows_send[...] = jnp.dot(hidden, wdn[:, theirs], preferred_element_type=f32).astype(bf16)
-    trade = pltpu.make_async_remote_copy(
-        src_ref=rows_send, dst_ref=rows_recv, send_sem=x_sem.at[2], recv_sem=x_sem.at[3],
-        device_id={"head": 1 - h}, device_id_type=MESH,
-    )
-    trade.start()
     own = jnp.dot(hidden, wdn[:, ours], preferred_element_type=f32)
     dest = lax.broadcasted_iota(jnp.int32, (n * 2 * SLOTS, count), 0)
     from_row = lax.broadcasted_iota(jnp.int32, (n * 2 * SLOTS, count), 1)
     home = from_row == (dest % SLOTS) * n + dest // (2 * SLOTS)
     upper = (dest // SLOTS) % 2
-    trade.wait_recv()
-    summed = (own + rows_recv[...].astype(f32)).astype(bf16)
-    back = jnp.zeros((n * 2 * SLOTS, quarter), f32)
-    for a in range(2):
-        put = jnp.where(jnp.logical_and(home, upper == a), 1.0, 0.0).astype(bf16)
-        back += jnp.dot(put, summed[:, a * quarter : (a + 1) * quarter], preferred_element_type=f32)
-    back_out[...] = blocks_of(back, n)
-    exchange_start(back_out, back_in, b_send, b_recv)
-    back_in[me] = back_out[me]
-    exchange_recv(back_out, back_in, b_send, b_recv)
-
-    returned = rows_of(back_in[...])
+    puts = [
+        jnp.where(jnp.logical_and(home, upper == a), 1.0, 0.0).astype(bf16) for a in range(2)
+    ]
+    for p in range(PARTS):
+        trade(p).wait_recv()
+        summed = own[:, p * share_cols : (p + 1) * share_cols] + rows_recv[p].astype(f32)
+        summed = summed.astype(bf16)
+        back = jnp.dot(puts[0], summed[:, :piece], preferred_element_type=f32)
+        back = back + jnp.dot(puts[1], summed[:, piece:], preferred_element_type=f32)
+        back_out[p] = blocks_of(back, n)
+        exchange_start(back_out.at[p], back_in.at[p], b_send.at[p], b_recv.at[p])
+        back_in[p, me] = back_out[p, me]
+
+    mixes = []
     for a in range(2):
         mix = jnp.where(part == a, blend, 0.0)
         high = mix.astype(bf16)
-        low = (mix - high.astype(f32)).astype(bf16)
-        added = jnp.dot(high, returned, preferred_element_type=f32)
-        added = added + jnp.dot(low, returned, preferred_element_type=f32)
-        start = pl.multiple_of(h * half + a * quarter, quarter)
-        out_ref[:, a * quarter : (a + 1) * quarter] = stream[:, pl.ds(start, quarter)] + added
+        mixes.append((high, (mix - high.astype(f32)).astype(bf16)))
+    for p in range(PARTS):
+        exchange_recv(back_out.at[p], back_in.at[p], b_send.at[p], b_recv.at[p])
+        returned = rows_of(back_in[p])
+        for a in range(2):
+            added = jnp.dot(mixes[a][0], returned, preferred_element_type=f32)
+            added = added + jnp.dot(mixes[a][1], returned, preferred_element_type=f32)
+            here = p * share_cols + a * piece
+            start = pl.multiple_of(h * half + here, piece)
+            out_ref[:, here : here + piece] = stream[:, pl.ds(start, piece)] + added
 
     for k in range(CHUNKS):
         drain(k)
-    t_drain(0)
     swap.wait_send()
-    trade.wait_send()
     exchange_sent(outgoing, incoming, a_send, a_recv)
-    exchange_sent(back_out, back_in, b_send, b_recv)
-
-
-def fused(latents, resid, norm_gain, route_ids, route_weights, w_value_out, w_gate_up, w_down):
+    for p in range(PARTS):
+        t_drain(p)
+        trade(p).wait_send()
+        exchange_sent(back_out.at[p], back_in.at[p], b_send.at[p], b_recv.at[p])
+
+
+def fused(q_latent, q_rotary, cache_latent, cache_rotary, lengths, resid, norm_gain, route_ids, route_weights, w_value_out,
+          w_gate_up, w_down):
     n = LINE * PAIR * CORE
     seqs, width = resid.shape
-    depth = latents.shape[1] // CHUNKS
+    head_count, latent = q_latent.shape[1:]
     cols = w_value_out.shape[1]
     half = width // 2
     capacity = -(-(seqs * route_ids.shape[1]) // n)
@@ -343,33 +383,39 @@
     return pl.pallas_call(
         layer_kernel,
         out_shape=jax.ShapeDtypeStruct((seqs, half), f32),
-        in_specs=[vmem] * 5 + [anywhere] * 3,
+        in_specs=[vmem] * 9 + [anywhere] * 3,
         out_specs=vmem,
         scratch_shapes=[
-            pltpu.VMEM(w_value_out.shape, bf16),
+            pltpu.VMEM(w_value_out.shape[::-1], bf16),
             pltpu.VMEM(gate_up.shape, bf16),
             pltpu.VMEM(down.shape, bf16),
-            pltpu.VMEM((CHUNKS, n, seqs, depth), bf16),
+            pltpu.VMEM((head_count, seqs, latent), f32),
+            pltpu.VMEM((CHUNKS, n, head_count // CHUNKS, seqs, latent), bf16),
             pltpu.VMEM((n * seqs, cols), f32),
             pltpu.VMEM((n * seqs, cols), f32),
             pltpu.VMEM((n, seqs, cols), bf16),
             pltpu.VMEM((n, seqs, cols), bf16),
             pltpu.VMEM((seqs, width), f32),
-            pltpu.VMEM((1, n, seqs, width + EXTRA), bf16),
-            pltpu.VMEM((capacity * n, half), bf16),
-            pltpu.VMEM((capacity * n, half), bf16),
-            pltpu.VMEM((n, 2 * SLOTS, half // 2), bf16),
-            pltpu.VMEM((n, 2 * SLOTS, half // 2), bf16),
+            pltpu.VMEM((PARTS, n, seqs, width // PARTS + EXTRA), bf16),
+            pltpu.VMEM((PARTS, capacity * n, half // PARTS), bf16),
+            pltpu.VMEM((PARTS, capacity * n, half // PARTS), bf16),
+            pltpu.VMEM((PARTS, n, 2 * SLOTS, half // (2 * PARTS)), bf16),
+            pltpu.VMEM((PARTS, n, 2 * SLOTS, half // (2 * PARTS)), bf16),
             dma((3,)),
             dma((CHUNKS, LINE)), dma((CHUNKS, LINE)), dma((CHUNKS, LINE)),
             dma((CHUNKS, PAIR * LINE)), dma((CHUNKS, n)),
-            dma((1, LINE)), dma((1, LINE)), dma((1, LINE)), dma((1, PAIR * LINE)), dma((1, n)),
-            dma((4,)), dma((n,)), dma((n,)), dma((n,)), dma((n,)),
+            dma((PARTS, LINE)), dma((PARTS, LINE)), dma((PARTS, LINE)),
+            dma((PARTS, PAIR * LINE)), dma((PARTS, n)),
+            dma((2,)), dma((PARTS,)), dma((PARTS,)), dma((n,)), dma((n,)),
+            dma((PARTS, n)), dma((PARTS, n)),
         ],
         compiler_params=pltpu.CompilerParams(
             collective_id=0, has_side_effects=True, vmem_limit_bytes=56 * 1024 * 1024
         ),
-    )(latents, resid, norm_gain[None, :], route_ids, route_weights, w_value_out, gate_up, down)
+    )(
+        q_latent, q_rotary, cache_latent, cache_rotary, lengths[:, None], resid,
+        norm_gain[None, :], route_ids, route_weights, w_value_out.T, gate_up, down,
+    )
 
 
 def attend(q_latent, q_rotary, cache_latent, cache_rotary, lengths):
@@ -403,16 +449,17 @@
     w_down,
 ):
     seq_local = q_latent.shape[0]
-    latent_out = attend(q_latent, q_rotary, cache_latent, cache_rotary, lengths)
-    flattened = latent_out.reshape(seq_local, -1)
     if (
         lax.axis_size("head") == 2
         and lax.axis_size("expert") == LINE * PAIR * CORE
         and seq_local == 8
     ):
         return fused(
-            flattened, resid, norm_gain, route_ids, route_weights, w_value_out, w_gate_up, w_down
+            q_latent, q_rotary, cache_latent, cache_rotary, lengths, resid, norm_gain,
+            route_ids, route_weights, w_value_out, w_gate_up, w_down,
         )
+    latent_out = attend(q_latent, q_rotary, cache_latent, cache_rotary, lengths)
+    flattened = latent_out.reshape(seq_local, -1)
     column_terms = jnp.dot(
         lax.all_gather(flattened, "expert", axis=0, tiled=True),
         w_value_out,

time: 107 us -> 86.5 us (0.81); the launches traced: 106 us -> 86.3 us
  local copies, waits for them, and re-layouts: 18.6 us -> 2.85 us
  matrix products: 2.97 us -> 0 us
    unnamed x5 -> x1, local copies, waits for them, and re-layouts: 18.6 us -> 1.53 us
    dot_general x3 -> x0, matrix products: 2.97 us -> none  [the longest x1 1.38 us: attend(): jnp.einsum('shl,scl->shc', q_latent, cache_latent, preferred_element_type...]
    broadcast_in_dim x0 -> x1, local copies, waits for them, and re-layouts: none -> 1.32 us  [fused(): lengths[:, None]]
where the time goes in v2:
time: 86.5 us; the launch traced here: 86.3 us
  Pallas kernels  83.5 us (97%)
  local copies, waits for them, and re-layouts  2.85 us (3%)
    pallas_call x1, Pallas kernels, fused(): pl.pallas_call(layer_kernel, out_shape=jax.ShapeDtypeStruct((seqs, half),...  83.5 us

profile of v2, /device:TPU:0, one launch (start us, length us, event | category | flops | bytes accessed | tf_op | source)
XLA Modules:
  0.0 86.3 jit_solution(4155654921569049271)
XLA Ops:
  0.0 1.3 %copy.13.len_ref = s32[8,1]{1,0:T(8,128)} copy(s32[8,1]{0,1:T(1,128)} %bitcast.9) | data formatting | bytes 64 | tf_op jit(solution)/shard_map/broadcast_in_dim | solution.py:416
  1.3 83.5 %shard_map.118 = f32[8,2560]{1,0:T(8,128)} custom-call(bf16[8,32,512]{2,1,0:T(8,128)(2,1)} %q_ref.1, bf16[8,32,64]{2,1,0:T(8,128)(2,1)} %qr_ref.1, bf16[8,128,512]{2,1,0:T(8,128)(2,1)} %cache_ref.1, bf16[8,64,128]{2,1,0:T(8,128)(2,1)} %rot_ref.1, s32[8,1]{1,0:T(8,128)} %copy.13.len_ref, bf16[8,5120]{1,0:T(8,128)(2,1)} %resid_ref.1, f32[1,5120]{1,0:T(1,128)} %bitcast.8, ...), custom_call_target="tpu_custom_call" | custom-call | tf_op jit(solution)/shard_map/pallas_call | solution.py:383
  84.8 1.5 %copy.15 = f32[8,2560]{1,0:T(8,128)} copy(f32[8,2560]{1,0:T(8,128)} %shard_map.118) | data formatting | bytes 163840

commit v3 on v2

--- a/solution.py
+++ b/solution.py
@@ -14,7 +14,7 @@
 LINE, PAIR, CORE = 4, 2, 2
 CHUNKS = 4
 EXTRA = 128
-SLOTS = 4
+ROWS = 16
 PARTS = 2
 
 
@@ -27,7 +27,7 @@
     return rows.reshape(n, rows.shape[0] // n, rows.shape[1]).astype(jnp.bfloat16)
 
 
-def spread(z, y, c, buffers, up, down, side, sib, recv):
+def spread(z, y, c, far, buffers, up, down, side, sib, recv):
     def slot(zz, yy, cc):
         return (zz * PAIR + yy) * CORE + cc
 
@@ -52,8 +52,27 @@
         def _():
             act(copy(k, s, down, zz, slot(z - 1, y, c)))
 
-        act(copy(k, s, side, zz, slot(z, 1 - y, c)))
+        ends = jnp.logical_or(zz == 0, zz == LINE - 1)
+        along = jnp.logical_and(jnp.logical_and(k < far, ends), zz != z)
+
+        @pl.when(jnp.logical_not(along))
+        def _():
+            act(copy(k, s, side, zz, slot(z, 1 - y, c)))
+
         act(copy(k, s, sib, zz, slot(z, y, 1 - c)))
+
+    def each_across(k, zz, act):
+        s = slot(zz, 1 - y, c)
+
+        @pl.when(jnp.logical_and(k < far, jnp.logical_and(zz == 0, z < LINE - 1)))
+        def _():
+            act(copy(k, s, up, LINE + zz, slot(z + 1, y, c)))
+
+        @pl.when(jnp.logical_and(k < far, jnp.logical_and(zz == LINE - 1, z > 0)))
+        def _():
+            act(copy(k, s, down, LINE + zz, slot(z - 1, y, c)))
+
+        act(copy(k, s, sib, LINE + zz, slot(z, y, 1 - c)))
 
     def arrived(k, s):
         copy(k, s, sib, 0, slot(z, y, 1 - c)).wait_recv()
@@ -78,9 +97,8 @@
             each_send(k, zz, lambda x: x.start())
 
         def across(zz):
-            s = slot(zz, 1 - y, c)
-            arrived(k, s)
-            copy(k, s, sib, LINE + zz, slot(z, y, 1 - c)).start()
+            arrived(k, slot(zz, 1 - y, c))
+            each_across(k, zz, lambda x: x.start())
 
         if d < LINE:
             at_distance(d, line)
@@ -97,7 +115,7 @@
     def drain(k):
         def body(zz, carry):
             each_send(k, zz, lambda x: x.wait_send())
-            copy(k, slot(zz, 1 - y, c), sib, LINE + zz, slot(z, y, 1 - c)).wait_send()
+            each_across(k, zz, lambda x: x.wait_send())
             return carry
 
         lax.fori_loop(0, LINE, body, 0)
@@ -108,7 +126,7 @@
 def layer_kernel(
     q_ref, qr_ref, cache_ref, rot_ref, len_ref, resid_ref, gain_ref, ids_ref, weights_ref, wvo_hbm, wgu_hbm, wdn_hbm,
     out_ref,
-    wvo, wgu, wdn, heads, gathered, partial, partner, outgoing, incoming, stream,
+    wvo, wgu, wdn, heads, gathered, partial, partner, last, last_partner, outgoing, incoming, stream,
     tokens, rows_send, rows_recv, back_out, back_in,
     w_sem, g_up, g_down, g_side, g_sib, g_recv, t_up, t_down, t_side, t_sib, t_recv,
     x_sem, y_send, y_recv, a_send, a_recv, b_send, b_recv,
@@ -118,12 +136,13 @@
     z, y, c = lax.div(me, PAIR * CORE), lax.rem(lax.div(me, CORE), PAIR), lax.rem(me, CORE)
     seqs, width = resid_ref.shape
     per_chunk, latent = gathered.shape[2], gathered.shape[4]
-    cols = partial.shape[1]
+    cols = partial.shape[2]
     half = out_ref.shape[1]
-    piece = half // (PARTS * 2)
     span = width // PARTS
     top = ids_ref.shape[1]
     capacity = rows_send.shape[1] // n
+    pieces = ROWS // capacity
+    piece = half // (PARTS * pieces)
     f32, bf16 = jnp.float32, jnp.bfloat16
 
     loads = [
@@ -146,22 +165,34 @@
 
     count = q_ref.shape[1]
     slot = lax.broadcasted_iota(jnp.int32, (count, cache_ref.shape[1]), 1)
+    parts = []
     for s in range(seqs):
-        cache = cache_ref[s]
         scores = lax.dot_general(
-            q_ref[s], cache, (((1,), (1,)), ((), ())), preferred_element_type=f32
+            q_ref[s], cache_ref[s], (((1,), (1,)), ((), ())), preferred_element_type=f32
         )
         scores = scores + jnp.dot(qr_ref[s], rot_ref[s], preferred_element_type=f32)
-        scores = jnp.where(slot < len_ref[s : s + 1, :], scores * softmax_scale, -1e30)
-        raised = jnp.exp(scores - jnp.max(scores, axis=1, keepdims=True))
-        probs = (raised / jnp.sum(raised, axis=1, keepdims=True)).astype(bf16)
-        heads[:, s, :] = jnp.dot(probs, cache, preferred_element_type=f32)
+        parts.append(jnp.where(slot < len_ref[s], scores * softmax_scale, -1e30))
+    scores = jnp.concatenate(parts, axis=0)
+    raised = jnp.exp(scores - jnp.max(scores, axis=1, keepdims=True))
+    probs = (raised / jnp.sum(raised, axis=1, keepdims=True)).astype(bf16)
+    for s in range(seqs):
+        heads[:, s, :] = jnp.dot(
+            probs[s * count : (s + 1) * count], cache_ref[s], preferred_element_type=f32
+        )
     for k in range(CHUNKS):
         gathered[k, me] = heads[k * per_chunk : (k + 1) * per_chunk].astype(bf16)
     partial[...] = jnp.zeros_like(partial)
     pl.semaphore_wait(barrier, n)
 
-    step, finish, drain = spread(z, y, c, gathered, g_up, g_down, g_side, g_sib, g_recv)
+    step, finish, drain = spread(z, y, c, CHUNKS // 2, gathered, g_up, g_down, g_side, g_sib, g_recv)
+    swap = pltpu.make_async_remote_copy(
+        src_ref=partial.at[0], dst_ref=partner, send_sem=x_sem.at[0], recv_sem=x_sem.at[1],
+        device_id={"head": 1 - h}, device_id_type=MESH,
+    )
+    swap_last = pltpu.make_async_remote_copy(
+        src_ref=last, dst_ref=last_partner, send_sem=x_sem.at[2], recv_sem=x_sem.at[3],
+        device_id={"head": 1 - h}, device_id_type=MESH,
+    )
     step(0, 0)
     step(1, 0)
 
@@ -181,27 +212,33 @@
         def _():
             k = t - LINE
             finish(k)
+            total = partial.at[k // (CHUNKS - 1)]
             for j in range(0, per_chunk, 2):
                 x = jnp.concatenate(
                     [rows_of(gathered[k, :, j]), rows_of(gathered[k, :, j + 1])], axis=1
                 )
                 start = pl.multiple_of((k * per_chunk + j) * latent, 2 * latent)
-                partial[...] += lax.dot_general(
+                total[...] += lax.dot_general(
                     x, wvo[:, pl.ds(start, 2 * latent)], (((1,), (1,)), ((), ())),
                     preferred_element_type=f32,
                 )
 
+            @pl.when(k == CHUNKS - 2)
+            def _():
+                swap.start()
+
         return carry
 
     lax.fori_loop(1, CHUNKS + LINE, turn, 0)
 
-    swap = pltpu.make_async_remote_copy(
-        src_ref=partial, dst_ref=partner, send_sem=x_sem.at[0], recv_sem=x_sem.at[1],
-        device_id={"head": 1 - h}, device_id_type=MESH,
-    )
-    swap.start()
+    last[...] = partial[1].astype(bf16)
+    swap_last.start()
+    for k in range(CHUNKS):
+        drain(k)
     swap.wait_recv()
-    outgoing[...] = blocks_of(partial[...] + partner[...], n)
+    sums = partial[0] + partial[1] + partner[...]
+    swap_last.wait_recv()
+    outgoing[...] = blocks_of(sums + last_partner[...].astype(f32), n)
 
     def owner(o, source, target, send, recv):
         to = lax.rem(me + o, n)
@@ -254,14 +291,14 @@
         tokens[k, me, :, :span] = normed[:, k * span : (k + 1) * span].astype(bf16)
         tokens[k, me, :, span:] = named.astype(bf16)
 
-    t_step, t_finish, t_drain = spread(z, y, c, tokens, t_up, t_down, t_side, t_sib, t_recv)
+    t_step, t_finish, t_drain = spread(z, y, c, PARTS // 2, tokens, t_up, t_down, t_side, t_sib, t_recv)
     for d in range(LINE + 1):
         for k in range(PARTS):
             t_step(k, d)
 
-    wide = n * 2 * SLOTS
+    wide = n * ROWS
     place = lax.broadcasted_iota(jnp.int32, (seqs, wide), 1)
-    which, part, at = place // (2 * SLOTS), (place // SLOTS) % 2, place % SLOTS
+    which, at = place // ROWS, place % ROWS
     hit = jnp.zeros((seqs, wide), f32)
     share = jnp.zeros((seqs, wide), f32)
     for k in range(top):
@@ -272,7 +309,14 @@
     rank = jnp.zeros((seqs, wide), f32)
     for t in range(seqs - 1):
         rank = rank + jnp.where(token > t, hit[t : t + 1, :], 0.0)
-    blend = jnp.where(rank == at.astype(f32), share, 0.0)
+    mixes = []
+    for a in range(pieces):
+        mix = jnp.where(rank == (at - a * capacity).astype(f32), share, 0.0)
+        high = mix.astype(bf16)
+        mixes.append((high, (mix - high.astype(f32)).astype(bf16)))
+    swap.wait_send()
+    swap_last.wait_send()
+    exchange_sent(outgoing, incoming, a_send, a_recv)
 
     t_finish(0)
     loads[1].wait()
@@ -326,44 +370,35 @@
         trade(p).start()
     ours = pl.ds(pl.multiple_of(h * half, half), half)
     own = jnp.dot(hidden, wdn[:, ours], preferred_element_type=f32)
-    dest = lax.broadcasted_iota(jnp.int32, (n * 2 * SLOTS, count), 0)
-    from_row = lax.broadcasted_iota(jnp.int32, (n * 2 * SLOTS, count), 1)
-    home = from_row == (dest % SLOTS) * n + dest // (2 * SLOTS)
-    upper = (dest // SLOTS) % 2
-    puts = [
-        jnp.where(jnp.logical_and(home, upper == a), 1.0, 0.0).astype(bf16) for a in range(2)
-    ]
+    dest = lax.broadcasted_iota(jnp.int32, (wide, count), 0)
+    from_row = lax.broadcasted_iota(jnp.int32, (wide, count), 1)
+    home = (from_row % n) * ROWS + from_row // n
+    puts = [jnp.where(dest == home + a * capacity, 1.0, 0.0).astype(bf16) for a in range(pieces)]
+    for p in range(PARTS):
+        t_drain(p)
     for p in range(PARTS):
         trade(p).wait_recv()
         summed = own[:, p * share_cols : (p + 1) * share_cols] + rows_recv[p].astype(f32)
         summed = summed.astype(bf16)
-        back = jnp.dot(puts[0], summed[:, :piece], preferred_element_type=f32)
-        back = back + jnp.dot(puts[1], summed[:, piece:], preferred_element_type=f32)
+        back = jnp.zeros((wide, piece), f32)
+        for a in range(pieces):
+            columns = summed[:, a * piece : (a + 1) * piece]
+            back = back + jnp.dot(puts[a], columns, preferred_element_type=f32)
         back_out[p] = blocks_of(back, n)
         exchange_start(back_out.at[p], back_in.at[p], b_send.at[p], b_recv.at[p])
         back_in[p, me] = back_out[p, me]
 
-    mixes = []
-    for a in range(2):
-        mix = jnp.where(part == a, blend, 0.0)
-        high = mix.astype(bf16)
-        mixes.append((high, (mix - high.astype(f32)).astype(bf16)))
     for p in range(PARTS):
         exchange_recv(back_out.at[p], back_in.at[p], b_send.at[p], b_recv.at[p])
         returned = rows_of(back_in[p])
-        for a in range(2):
+        for a in range(pieces):
             added = jnp.dot(mixes[a][0], returned, preferred_element_type=f32)
             added = added + jnp.dot(mixes[a][1], returned, preferred_element_type=f32)
             here = p * share_cols + a * piece
             start = pl.multiple_of(h * half + here, piece)
             out_ref[:, here : here + piece] = stream[:, pl.ds(start, piece)] + added
 
-    for k in range(CHUNKS):
-        drain(k)
-    swap.wait_send()
-    exchange_sent(outgoing, incoming, a_send, a_recv)
     for p in range(PARTS):
-        t_drain(p)
         trade(p).wait_send()
         exchange_sent(back_out.at[p], back_in.at[p], b_send.at[p], b_recv.at[p])
 
@@ -383,7 +418,7 @@
     return pl.pallas_call(
         layer_kernel,
         out_shape=jax.ShapeDtypeStruct((seqs, half), f32),
-        in_specs=[vmem] * 9 + [anywhere] * 3,
+        in_specs=[vmem] * 4 + [pl.BlockSpec(memory_space=pltpu.SMEM)] + [vmem] * 4 + [anywhere] * 3,
         out_specs=vmem,
         scratch_shapes=[
             pltpu.VMEM(w_value_out.shape[::-1], bf16),
@@ -391,29 +426,31 @@
             pltpu.VMEM(down.shape, bf16),
             pltpu.VMEM((head_count, seqs, latent), f32),
             pltpu.VMEM((CHUNKS, n, head_count // CHUNKS, seqs, latent), bf16),
+            pltpu.VMEM((2, n * seqs, cols), f32),
             pltpu.VMEM((n * seqs, cols), f32),
-            pltpu.VMEM((n * seqs, cols), f32),
+            pltpu.VMEM((n * seqs, cols), bf16),
+            pltpu.VMEM((n * seqs, cols), bf16),
             pltpu.VMEM((n, seqs, cols), bf16),
             pltpu.VMEM((n, seqs, cols), bf16),
             pltpu.VMEM((seqs, width), f32),
             pltpu.VMEM((PARTS, n, seqs, width // PARTS + EXTRA), bf16),
             pltpu.VMEM((PARTS, capacity * n, half // PARTS), bf16),
             pltpu.VMEM((PARTS, capacity * n, half // PARTS), bf16),
-            pltpu.VMEM((PARTS, n, 2 * SLOTS, half // (2 * PARTS)), bf16),
-            pltpu.VMEM((PARTS, n, 2 * SLOTS, half // (2 * PARTS)), bf16),
+            pltpu.VMEM((PARTS, n, ROWS, half // (PARTS * (ROWS // capacity))), bf16),
+            pltpu.VMEM((PARTS, n, ROWS, half // (PARTS * (ROWS // capacity))), bf16),
             dma((3,)),
-            dma((CHUNKS, LINE)), dma((CHUNKS, LINE)), dma((CHUNKS, LINE)),
+            dma((CHUNKS, PAIR * LINE)), dma((CHUNKS, PAIR * LINE)), dma((CHUNKS, LINE)),
             dma((CHUNKS, PAIR * LINE)), dma((CHUNKS, n)),
-            dma((PARTS, LINE)), dma((PARTS, LINE)), dma((PARTS, LINE)),
+            dma((PARTS, PAIR * LINE)), dma((PARTS, PAIR * LINE)), dma((PARTS, LINE)),
             dma((PARTS, PAIR * LINE)), dma((PARTS, n)),
-            dma((2,)), dma((PARTS,)), dma((PARTS,)), dma((n,)), dma((n,)),
+            dma((4,)), dma((PARTS,)), dma((PARTS,)), dma((n,)), dma((n,)),
             dma((PARTS, n)), dma((PARTS, n)),
         ],
         compiler_params=pltpu.CompilerParams(
             collective_id=0, has_side_effects=True, vmem_limit_bytes=56 * 1024 * 1024
         ),
     )(
-        q_latent, q_rotary, cache_latent, cache_rotary, lengths[:, None], resid,
+        q_latent, q_rotary, cache_latent, cache_rotary, lengths, resid,
         norm_gain[None, :], route_ids, route_weights, w_value_out.T, gate_up, down,
     )
 

time: 86.5 us -> 81.2 us (0.939)
  Pallas kernels: 83.5 us -> 79.5 us
  local copies, waits for them, and re-layouts: 2.85 us -> 1.53 us
    pallas_call x1, Pallas kernels: 83.5 us -> 79.5 us  [fused(): pl.pallas_call(layer_kernel, out_shape=jax.ShapeDtypeStruct((seqs, half),...]
    broadcast_in_dim x1 -> x0, local copies, waits for them, and re-layouts: 1.32 us -> none  [fused(): lengths[:, None]]
where the time goes in v3:
time: 81.2 us; the launch traced here: 81 us
  Pallas kernels  79.5 us (98%)
  local copies, waits for them, and re-layouts  1.53 us (2%)
    pallas_call x1, Pallas kernels, fused(): pl.pallas_call(layer_kernel, out_shape=jax.ShapeDtypeStruct((seqs, half),...  79.5 us

profile of v3, /device:TPU:0, one launch (start us, length us, event | category | flops | bytes accessed | tf_op | source)
XLA Modules:
  0.0 81.0 jit_solution(9986666953279776896)
XLA Ops:
  0.0 79.5 %shard_map.118 = f32[8,2560]{1,0:T(8,128)} custom-call(bf16[8,32,512]{2,1,0:T(8,128)(2,1)} %q_ref.1, bf16[8,32,64]{2,1,0:T(8,128)(2,1)} %qr_ref.1, bf16[8,128,512]{2,1,0:T(8,128)(2,1)} %cache_ref.1, bf16[8,64,128]{2,1,0:T(8,128)(2,1)} %rot_ref.1, s32[8]{0:T(128)} %len_ref.1, bf16[8,5120]{1,0:T(8,128)(2,1)} %resid_ref.1, f32[1,5120]{1,0:T(1,128)} %bitcast.7, ...), custom_call_target="tpu_custom_call" | custom-call | tf_op jit(solution)/shard_map/pallas_call | solution.py:418
  79.5 1.5 %copy.14 = f32[8,2560]{1,0:T(8,128)} copy(f32[8,2560]{1,0:T(8,128)} %shard_map.118) | data formatting | bytes 163840

commit v4 on v3

--- a/solution.py
+++ b/solution.py
@@ -12,7 +12,7 @@
 norm_epsilon = 1e-06
 
 LINE, PAIR, CORE = 4, 2, 2
-CHUNKS = 4
+CHUNKS = 8
 EXTRA = 128
 ROWS = 16
 PARTS = 2

time: 81.2 us -> 91.6 us (1.13)
  Pallas kernels: 79.5 us -> 89.9 us
    pallas_call x1, Pallas kernels: 79.5 us -> 89.9 us  [fused(): pl.pallas_call(layer_kernel, out_shape=jax.ShapeDtypeStruct((seqs, half),...]
where the time goes in v4:
time: 91.6 us; the launch traced here: 91.4 us
  Pallas kernels  89.9 us (98%)
  local copies, waits for them, and re-layouts  1.53 us (2%)
    pallas_call x1, Pallas kernels, fused(): pl.pallas_call(layer_kernel, out_shape=jax.ShapeDtypeStruct((seqs, half),...  89.9 us

profile of v4, /device:TPU:0, one launch (start us, length us, event | category | flops | bytes accessed | tf_op | source)
XLA Modules:
  0.0 91.4 jit_solution(935908466003995454)
XLA Ops:
  0.0 89.9 %shard_map.118 = f32[8,2560]{1,0:T(8,128)} custom-call(bf16[8,32,512]{2,1,0:T(8,128)(2,1)} %q_ref.1, bf16[8,32,64]{2,1,0:T(8,128)(2,1)} %qr_ref.1, bf16[8,128,512]{2,1,0:T(8,128)(2,1)} %cache_ref.1, bf16[8,64,128]{2,1,0:T(8,128)(2,1)} %rot_ref.1, s32[8]{0:T(128)} %len_ref.1, bf16[8,5120]{1,0:T(8,128)(2,1)} %resid_ref.1, f32[1,5120]{1,0:T(1,128)} %bitcast.7, ...), custom_call_target="tpu_custom_call" | custom-call | tf_op jit(solution)/shard_map/pallas_call | solution.py:418
  89.9 1.5 %copy.14 = f32[8,2560]{1,0:T(8,128)} copy(f32[8,2560]{1,0:T(8,128)} %shard_map.118) | data formatting | bytes 163840

commit v5 on v3

--- a/solution.py
+++ b/solution.py
@@ -27,55 +27,68 @@
     return rows.reshape(n, rows.shape[0] // n, rows.shape[1]).astype(jnp.bfloat16)
 
 
+def device(zz, yy, cc):
+    return (zz * PAIR + yy) * CORE + cc
+
+
+def block_of(e):
+    cc, yy, zz = lax.rem(e, CORE), lax.rem(lax.div(e, CORE), PAIR), lax.div(e, PAIR * CORE)
+    return (cc * PAIR + yy) * LINE + zz
+
+
 def spread(z, y, c, far, buffers, up, down, side, sib, recv):
-    def slot(zz, yy, cc):
-        return (zz * PAIR + yy) * CORE + cc
+    def slot(zz, yy):
+        return (c * PAIR + yy) * LINE + zz
 
     def copy(k, s, sems, index, target):
         return pltpu.make_async_remote_copy(
             src_ref=buffers.at[k, s],
             dst_ref=buffers.at[k, s],
             send_sem=sems.at[k, index],
-            recv_sem=recv.at[k, s],
+            recv_sem=recv.at[k, lax.rem(s, PAIR * LINE)],
             device_id={"expert": target},
             device_id_type=MESH,
         )
 
+    def group(k, yy, core):
+        blocks = buffers.at[k, pl.ds((core * PAIR + yy) * LINE, LINE)]
+        return pltpu.make_async_remote_copy(
+            src_ref=blocks, dst_ref=blocks, send_sem=sib.at[k, yy],
+            recv_sem=recv.at[k, PAIR * LINE + yy],
+            device_id={"expert": device(z, y, 1 - c)}, device_id_type=MESH,
+        )
+
     def each_send(k, zz, act):
-        s = slot(zz, y, c)
+        s = slot(zz, y)
 
         @pl.when(jnp.logical_and(zz <= z, z < LINE - 1))
         def _():
-            act(copy(k, s, up, zz, slot(z + 1, y, c)))
+            act(copy(k, s, up, zz, device(z + 1, y, c)))
 
         @pl.when(jnp.logical_and(zz >= z, z > 0))
         def _():
-            act(copy(k, s, down, zz, slot(z - 1, y, c)))
+            act(copy(k, s, down, zz, device(z - 1, y, c)))
 
         ends = jnp.logical_or(zz == 0, zz == LINE - 1)
         along = jnp.logical_and(jnp.logical_and(k < far, ends), zz != z)
 
         @pl.when(jnp.logical_not(along))
         def _():
-            act(copy(k, s, side, zz, slot(z, 1 - y, c)))
-
-        act(copy(k, s, sib, zz, slot(z, y, 1 - c)))
+            act(copy(k, s, side, zz, device(z, 1 - y, c)))
 
     def each_across(k, zz, act):
-        s = slot(zz, 1 - y, c)
+        s = slot(zz, 1 - y)
 
         @pl.when(jnp.logical_and(k < far, jnp.logical_and(zz == 0, z < LINE - 1)))
         def _():
-            act(copy(k, s, up, LINE + zz, slot(z + 1, y, c)))
+            act(copy(k, s, up, LINE + zz, device(z + 1, y, c)))
 
         @pl.when(jnp.logical_and(k < far, jnp.logical_and(zz == LINE - 1, z > 0)))
         def _():
-            act(copy(k, s, down, LINE + zz, slot(z - 1, y, c)))
-
-        act(copy(k, s, sib, LINE + zz, slot(z, y, 1 - c)))
+            act(copy(k, s, down, LINE + zz, device(z - 1, y, c)))
 
     def arrived(k, s):
-        copy(k, s, sib, 0, slot(z, y, 1 - c)).wait_recv()
+        copy(k, s, side, 0, device(z, 1 - y, c)).wait_recv()
 
     def at_distance(d, act):
         if d == 0:
@@ -93,24 +106,25 @@
     def step(k, d):
         def line(zz):
             if d > 0:
-                arrived(k, slot(zz, y, c))
+                arrived(k, slot(zz, y))
             each_send(k, zz, lambda x: x.start())
 
         def across(zz):
-            arrived(k, slot(zz, 1 - y, c))
+            arrived(k, slot(zz, 1 - y))
             each_across(k, zz, lambda x: x.start())
 
         if d < LINE:
             at_distance(d, line)
+        if d == LINE - 1:
+            group(k, y, c).start()
         if d > 0:
             at_distance(d - 1, across)
+        if d == LINE:
+            group(k, 1 - y, c).start()
 
     def finish(k):
-        def body(i, carry):
-            arrived(k, slot(lax.div(i, PAIR), lax.rem(i, PAIR), 1 - c))
-            return carry
-
-        lax.fori_loop(0, LINE * PAIR, body, 0)
+        group(k, y, 1 - c).wait_recv()
+        group(k, 1 - y, 1 - c).wait_recv()
 
     def drain(k):
         def body(zz, carry):
@@ -119,6 +133,8 @@
             return carry
 
         lax.fori_loop(0, LINE, body, 0)
+        group(k, y, c).wait_send()
+        group(k, 1 - y, c).wait_send()
 
     return step, finish, drain
 
@@ -134,6 +150,7 @@
     n = LINE * PAIR * CORE
     h, me = lax.axis_index("head"), lax.axis_index("expert")
     z, y, c = lax.div(me, PAIR * CORE), lax.rem(lax.div(me, CORE), PAIR), lax.rem(me, CORE)
+    here = block_of(me)
     seqs, width = resid_ref.shape
     per_chunk, latent = gathered.shape[2], gathered.shape[4]
     cols = partial.shape[2]
@@ -180,7 +197,7 @@
             probs[s * count : (s + 1) * count], cache_ref[s], preferred_element_type=f32
         )
     for k in range(CHUNKS):
-        gathered[k, me] = heads[k * per_chunk : (k + 1) * per_chunk].astype(bf16)
+        gathered[k, here] = heads[k * per_chunk : (k + 1) * per_chunk].astype(bf16)
     partial[...] = jnp.zeros_like(partial)
     pl.semaphore_wait(barrier, n)
 
@@ -243,7 +260,7 @@
     def owner(o, source, target, send, recv):
         to = lax.rem(me + o, n)
         return pltpu.make_async_remote_copy(
-            src_ref=source.at[to], dst_ref=target.at[me], send_sem=send.at[to],
+            src_ref=source.at[block_of(to)], dst_ref=target.at[me], send_sem=send.at[to],
             recv_sem=recv.at[me], device_id={"expert": to}, device_id_type=MESH,
         )
 
@@ -258,7 +275,7 @@
         def body(o, carry):
             who = lax.rem(me + o, n)
             pltpu.make_async_remote_copy(
-                src_ref=source.at[who], dst_ref=target.at[who], send_sem=send.at[who],
+                src_ref=source.at[block_of(who)], dst_ref=target.at[who], send_sem=send.at[who],
                 recv_sem=recv.at[who], device_id={"expert": who}, device_id_type=MESH,
             ).wait_recv()
             return carry
@@ -273,7 +290,7 @@
         lax.fori_loop(1, n, body, 0)
 
     exchange_start(outgoing, incoming, a_send, a_recv)
-    incoming[me] = outgoing[me]
+    incoming[me] = outgoing[here]
     ids = ids_ref[...]
     lane = lax.broadcasted_iota(jnp.int32, (seqs, EXTRA), 1)
     named = jnp.zeros((seqs, EXTRA), f32)
@@ -288,8 +305,8 @@
     mean_square = jnp.sum(rows * rows, axis=1, keepdims=True) * (1.0 / width)
     normed = rows * lax.rsqrt(mean_square + norm_epsilon) * gain_ref[...]
     for k in range(PARTS):
-        tokens[k, me, :, :span] = normed[:, k * span : (k + 1) * span].astype(bf16)
-        tokens[k, me, :, span:] = named.astype(bf16)
+        tokens[k, here, :, :span] = normed[:, k * span : (k + 1) * span].astype(bf16)
+        tokens[k, here, :, span:] = named.astype(bf16)
 
     t_step, t_finish, t_drain = spread(z, y, c, PARTS // 2, tokens, t_up, t_down, t_side, t_sib, t_recv)
     for d in range(LINE + 1):
@@ -386,7 +403,7 @@
             back = back + jnp.dot(puts[a], columns, preferred_element_type=f32)
         back_out[p] = blocks_of(back, n)
         exchange_start(back_out.at[p], back_in.at[p], b_send.at[p], b_recv.at[p])
-        back_in[p, me] = back_out[p, me]
+        back_in[p, me] = back_out[p, here]
 
     for p in range(PARTS):
         exchange_recv(back_out.at[p], back_in.at[p], b_send.at[p], b_recv.at[p])
@@ -394,9 +411,9 @@
         for a in range(pieces):
             added = jnp.dot(mixes[a][0], returned, preferred_element_type=f32)
             added = added + jnp.dot(mixes[a][1], returned, preferred_element_type=f32)
-            here = p * share_cols + a * piece
-            start = pl.multiple_of(h * half + here, piece)
-            out_ref[:, here : here + piece] = stream[:, pl.ds(start, piece)] + added
+            at = p * share_cols + a * piece
+            start = pl.multiple_of(h * half + at, piece)
+            out_ref[:, at : at + piece] = stream[:, pl.ds(start, piece)] + added
 
     for p in range(PARTS):
         trade(p).wait_send()
@@ -440,9 +457,9 @@
             pltpu.VMEM((PARTS, n, ROWS, half // (PARTS * (ROWS // capacity))), bf16),
             dma((3,)),
             dma((CHUNKS, PAIR * LINE)), dma((CHUNKS, PAIR * LINE)), dma((CHUNKS, LINE)),
-            dma((CHUNKS, PAIR * LINE)), dma((CHUNKS, n)),
+            dma((CHUNKS, PAIR)), dma((CHUNKS, PAIR * LINE + PAIR)),
             dma((PARTS, PAIR * LINE)), dma((PARTS, PAIR * LINE)), dma((PARTS, LINE)),
-            dma((PARTS, PAIR * LINE)), dma((PARTS, n)),
+            dma((PARTS, PAIR)), dma((PARTS, PAIR * LINE + PAIR)),
             dma((4,)), dma((PARTS,)), dma((PARTS,)), dma((n,)), dma((n,)),
             dma((PARTS, n)), dma((PARTS, n)),
         ],

time: 81.2 us -> 80.9 us (level)
  no operation moved by 1% of the time
where the time goes in v5:
time: 80.9 us; the launch traced here: 80.7 us
  Pallas kernels  79.2 us (98%)
  local copies, waits for them, and re-layouts  1.53 us (2%)
    pallas_call x1, Pallas kernels, fused(): pl.pallas_call(layer_kernel, out_shape=jax.ShapeDtypeStruct((seqs, half),...  79.2 us

profile of v5, /device:TPU:0, one launch (start us, length us, event | category | flops | bytes accessed | tf_op | source)
XLA Modules:
  0.0 80.7 jit_solution(17327009011262368436)
XLA Ops:
  0.0 79.2 %shard_map.118 = f32[8,2560]{1,0:T(8,128)} custom-call(bf16[8,32,512]{2,1,0:T(8,128)(2,1)} %q_ref.1, bf16[8,32,64]{2,1,0:T(8,128)(2,1)} %qr_ref.1, bf16[8,128,512]{2,1,0:T(8,128)(2,1)} %cache_ref.1, bf16[8,64,128]{2,1,0:T(8,128)(2,1)} %rot_ref.1, s32[8]{0:T(128)} %len_ref.1, bf16[8,5120]{1,0:T(8,128)(2,1)} %resid_ref.1, f32[1,5120]{1,0:T(1,128)} %bitcast.7, ...), custom_call_target="tpu_custom_call" | custom-call | tf_op jit(solution)/shard_map/pallas_call | solution.py:435
  79.2 1.5 %copy.14 = f32[8,2560]{1,0:T(8,128)} copy(f32[8,2560]{1,0:T(8,128)} %shard_map.118) | data formatting | bytes 163840

commit v6 on v5

--- a/solution.py
+++ b/solution.py
@@ -12,7 +12,7 @@
 norm_epsilon = 1e-06
 
 LINE, PAIR, CORE = 4, 2, 2
-CHUNKS = 4
+CHUNKS = 2
 EXTRA = 128
 ROWS = 16
 PARTS = 2

time: 80.9 us -> 78.7 us (0.973)
  Pallas kernels: 79.2 us -> 77 us
    pallas_call x1, Pallas kernels: 79.2 us -> 77 us  [fused(): pl.pallas_call(layer_kernel, out_shape=jax.ShapeDtypeStruct((seqs, half),...]
where the time goes in v6:
time: 78.7 us; the launch traced here: 78.5 us
  Pallas kernels  77 us (98%)
  local copies, waits for them, and re-layouts  1.53 us (2%)
    pallas_call x1, Pallas kernels, fused(): pl.pallas_call(layer_kernel, out_shape=jax.ShapeDtypeStruct((seqs, half),...  77 us

profile of v6, /device:TPU:0, one launch (start us, length us, event | category | flops | bytes accessed | tf_op | source)
XLA Modules:
  0.0 78.5 jit_solution(1738593159509660966)
XLA Ops:
  0.0 77.0 %shard_map.118 = f32[8,2560]{1,0:T(8,128)} custom-call(bf16[8,32,512]{2,1,0:T(8,128)(2,1)} %q_ref.1, bf16[8,32,64]{2,1,0:T(8,128)(2,1)} %qr_ref.1, bf16[8,128,512]{2,1,0:T(8,128)(2,1)} %cache_ref.1, bf16[8,64,128]{2,1,0:T(8,128)(2,1)} %rot_ref.1, s32[8]{0:T(128)} %len_ref.1, bf16[8,5120]{1,0:T(8,128)(2,1)} %resid_ref.1, f32[1,5120]{1,0:T(1,128)} %bitcast.7, ...), custom_call_target="tpu_custom_call" | custom-call | tf_op jit(solution)/shard_map/pallas_call | solution.py:435
  77.0 1.5 %copy.14 = f32[8,2560]{1,0:T(8,128)} copy(f32[8,2560]{1,0:T(8,128)} %shard_map.118) | data formatting | bytes 163840

commit v7 on v6

--- a/solution.py
+++ b/solution.py
@@ -153,7 +153,7 @@
     here = block_of(me)
     seqs, width = resid_ref.shape
     per_chunk, latent = gathered.shape[2], gathered.shape[4]
-    cols = partial.shape[2]
+    cols = partial.shape[1]
     half = out_ref.shape[1]
     span = width // PARTS
     top = ids_ref.shape[1]
@@ -236,7 +236,7 @@
                 )
                 start = pl.multiple_of((k * per_chunk + j) * latent, 2 * latent)
                 total[...] += lax.dot_general(
-                    x, wvo[:, pl.ds(start, 2 * latent)], (((1,), (1,)), ((), ())),
+                    wvo[:, pl.ds(start, 2 * latent)], x, (((1,), (1,)), ((), ())),
                     preferred_element_type=f32,
                 )
 
@@ -255,7 +255,7 @@
     swap.wait_recv()
     sums = partial[0] + partial[1] + partner[...]
     swap_last.wait_recv()
-    outgoing[...] = blocks_of(sums + last_partner[...].astype(f32), n)
+    outgoing[...] = blocks_of((sums + last_partner[...].astype(f32)).T, n)
 
     def owner(o, source, target, send, recv):
         to = lax.rem(me + o, n)
@@ -443,10 +443,10 @@
             pltpu.VMEM(down.shape, bf16),
             pltpu.VMEM((head_count, seqs, latent), f32),
             pltpu.VMEM((CHUNKS, n, head_count // CHUNKS, seqs, latent), bf16),
-            pltpu.VMEM((2, n * seqs, cols), f32),
-            pltpu.VMEM((n * seqs, cols), f32),
-            pltpu.VMEM((n * seqs, cols), bf16),
-            pltpu.VMEM((n * seqs, cols), bf16),
+            pltpu.VMEM((2, cols, n * seqs), f32),
+            pltpu.VMEM((cols, n * seqs), f32),
+            pltpu.VMEM((cols, n * seqs), bf16),
+            pltpu.VMEM((cols, n * seqs), bf16),
             pltpu.VMEM((n, seqs, cols), bf16),
             pltpu.VMEM((n, seqs, cols), bf16),
             pltpu.VMEM((seqs, width), f32),

time: 78.7 us -> 77.8 us (0.989)
  Pallas kernels: 77 us -> 76.1 us
    pallas_call x1, Pallas kernels: 77 us -> 76.1 us  [fused(): pl.pallas_call(layer_kernel, out_shape=jax.ShapeDtypeStruct((seqs, half),...]
where the time goes in v7:
time: 77.8 us; the launch traced here: 77.6 us
  Pallas kernels  76.1 us (98%)
  local copies, waits for them, and re-layouts  1.53 us (2%)
    pallas_call x1, Pallas kernels, fused(): pl.pallas_call(layer_kernel, out_shape=jax.ShapeDtypeStruct((seqs, half),...  76.1 us

profile of v7, /device:TPU:0, one launch (start us, length us, event | category | flops | bytes accessed | tf_op | source)
XLA Modules:
  0.0 77.6 jit_solution(16616869687309922260)
XLA Ops:
  0.0 76.1 %shard_map.118 = f32[8,2560]{1,0:T(8,128)} custom-call(bf16[8,32,512]{2,1,0:T(8,128)(2,1)} %q_ref.1, bf16[8,32,64]{2,1,0:T(8,128)(2,1)} %qr_ref.1, bf16[8,128,512]{2,1,0:T(8,128)(2,1)} %cache_ref.1, bf16[8,64,128]{2,1,0:T(8,128)(2,1)} %rot_ref.1, s32[8]{0:T(128)} %len_ref.1, bf16[8,5120]{1,0:T(8,128)(2,1)} %resid_ref.1, f32[1,5120]{1,0:T(1,128)} %bitcast.7, ...), custom_call_target="tpu_custom_call" | custom-call | tf_op jit(solution)/shard_map/pallas_call | solution.py:435
  76.1 1.5 %copy.14 = f32[8,2560]{1,0:T(8,128)} copy(f32[8,2560]{1,0:T(8,128)} %shard_map.118) | data formatting | bytes 163840

commit v8 on v7

--- a/solution.py
+++ b/solution.py
@@ -15,7 +15,7 @@
 CHUNKS = 2
 EXTRA = 128
 ROWS = 16
-PARTS = 2
+PARTS = 1
 
 
 def rows_of(blocks):

time: 77.8 us -> 78.8 us (1.013)
  Pallas kernels: 76.1 us -> 77 us
    pallas_call x1, Pallas kernels: 76.1 us -> 77 us  [fused(): pl.pallas_call(layer_kernel, out_shape=jax.ShapeDtypeStruct((seqs, half),...]
where the time goes in v8:
time: 78.8 us; the launch traced here: 78.6 us
  Pallas kernels  77 us (98%)
  local copies, waits for them, and re-layouts  1.53 us (2%)
    pallas_call x1, Pallas kernels, fused(): pl.pallas_call(layer_kernel, out_shape=jax.ShapeDtypeStruct((seqs, half),...  77 us

profile of v8, /device:TPU:0, one launch (start us, length us, event | category | flops | bytes accessed | tf_op | source)
XLA Modules:
  0.0 78.6 jit_solution(11111264016011121156)
XLA Ops:
  0.0 77.0 %shard_map.118 = f32[8,2560]{1,0:T(8,128)} custom-call(bf16[8,32,512]{2,1,0:T(8,128)(2,1)} %q_ref.1, bf16[8,32,64]{2,1,0:T(8,128)(2,1)} %qr_ref.1, bf16[8,128,512]{2,1,0:T(8,128)(2,1)} %cache_ref.1, bf16[8,64,128]{2,1,0:T(8,128)(2,1)} %rot_ref.1, s32[8]{0:T(128)} %len_ref.1, bf16[8,5120]{1,0:T(8,128)(2,1)} %resid_ref.1, f32[1,5120]{1,0:T(1,128)} %bitcast.7, ...), custom_call_target="tpu_custom_call" | custom-call | tf_op jit(solution)/shard_map/pallas_call | solution.py:435
  77.1 1.5 %copy.14 = f32[8,2560]{1,0:T(8,128)} copy(f32[8,2560]{1,0:T(8,128)} %shard_map.118) | data formatting | bytes 163840
